TPU v7x, 32 devices: a whole 2x2x4 slice. The times are simulated.
32 devices in a mesh: gx: 8 (over y, x, core), gy: 4 (over z).
Axes of the slice: x: 2, y: 2, z: 4, core: 2. Of those that a mesh axis runs over, the one named last changes fastest.
Arguments:
- rhs_field: float32 [3, 16, 128, 128], P(None, 'gx', 'gy'), may hold values from -6 to 6
- shear_modulus: float32 [16, 128, 128], P('gx', 'gy'), may hold values from 0.3 to 3
- lame_lambda: float32 [16, 128, 128], P('gx', 'gy'), may hold values from 0.3 to 3
- group_start: int32 [8, 4], P('gx'), may hold values from 0 to 1, as said below
Outputs:
- solution_field: float32 [3, 16, 128, 128], P(None, 'gx', 'gy')
- residual_field: float32 [3, 16, 128, 128], P(None, 'gx', 'gy')
Inputs may be any that keep to these rules, and one draw needn't show every extreme that they name: `group_start`: each index of gx has exactly one 1, at an index of gy from 1 to 3.
All inputs are finite; a program needn't handle non-finite values.
Results may differ from a plain program's by a relative error of at most 0.00011.
Values sent between devices are 32-bit elements; how exact they have to be, the bound alone decides.
A program may use at most 64 MiB of HBM per device.

v0:
```python
import jax
import jax.numpy as jnp
from jax import lax
from jax.sharding import PartitionSpec as P

SWEEPS = 3
COARSE_SWEEPS = 4


LOW_BOUND = 0.5
HIGH_BOUND = 6.0
SHIFT_SCALE = 48.0
UNITS = ((1, 0, 0), (0, 1, 0), (0, 0, 1))


def padded_2(block, sides, width):
    for axis, dim in sides:
        count = lax.axis_size(axis)
        forward = [(i, i + 1) for i in range(count - 1)]
        backward = [(target, source) for source, target in forward]
        low = lax.ppermute(
            lax.slice_in_dim(block, block.shape[dim] - width, None, axis=dim), axis, forward
        )
        high = lax.ppermute(lax.slice_in_dim(block, 0, width, axis=dim), axis, backward)
        block = jnp.concatenate([low, block, high], axis=dim)
    return block


def shifted(array, step_x, step_y, step_z):
    size_x = array.shape[-3] - 2
    size_y = array.shape[-2] - 2
    size_z = array.shape[-1] - 2
    return array[
        ...,
        1 + step_x : 1 + step_x + size_x,
        1 + step_y : 1 + step_y + size_y,
        1 + step_z : 1 + step_z + size_z,
    ]


def diagonal(mu_pad, lam_pad, scale):
    mu_centre = shifted(mu_pad, 0, 0, 0)
    lam_centre = shifted(lam_pad, 0, 0, 0)
    faces = 0.0
    for unit in UNITS:
        backward = tuple((-value for value in unit))
        faces = (
            faces
            + 0.5 * (mu_centre + shifted(mu_pad, *unit))
            + 0.5 * (mu_centre + shifted(mu_pad, *backward))
        )
    results = []
    for unit in UNITS:
        backward = tuple((-value for value in unit))
        results.append(scale * (faces + lam_centre + shifted(lam_pad, *backward)))
    return jnp.stack(results)


def operate(field_pad, mu_pad, lam_pad, scale):
    mu_centre = shifted(mu_pad, 0, 0, 0)
    lam_centre = shifted(lam_pad, 0, 0, 0)
    components = [field_pad[0], field_pad[1], field_pad[2]]
    centres = [shifted(value, 0, 0, 0) for value in components]
    laplace = [0.0, 0.0, 0.0]
    for unit in UNITS:
        backward = tuple((-value for value in unit))
        face_up = 0.5 * (mu_centre + shifted(mu_pad, *unit))
        face_down = 0.5 * (mu_centre + shifted(mu_pad, *backward))
        for comp_id in range(3):
            laplace[comp_id] = (
                laplace[comp_id]
                + face_up * (shifted(components[comp_id], *unit) - centres[comp_id])
                - face_down * (centres[comp_id] - shifted(components[comp_id], *backward))
            )

    def spread(offset):
        total = 0.0
        for comp_id in range(3):
            ahead = tuple((offset[axis_id] + UNITS[comp_id][axis_id] for axis_id in range(3)))
            total = total + (
                shifted(components[comp_id], *ahead) - shifted(components[comp_id], *offset)
            )
        return total

    stress_here = lam_centre * spread((0, 0, 0))
    results = []
    for comp_id in range(3):
        backward = tuple((-value for value in UNITS[comp_id]))
        grad_term = stress_here - shifted(lam_pad, *backward) * spread(backward)
        results.append(scale * (-laplace[comp_id] - grad_term))
    return jnp.stack(results)


def smooth(solution, residual, inverse_diag, apply_fn, steps):
    midpoint = 0.5 * (HIGH_BOUND + LOW_BOUND)
    halfwidth = 0.5 * (HIGH_BOUND - LOW_BOUND)
    sharpness = midpoint / halfwidth
    weight_old = 1.0 / sharpness
    direction = inverse_diag * residual / midpoint
    solution = solution + direction
    residual = residual - apply_fn(direction)
    for step_id in range(steps - 1):
        weight_new = 1.0 / (2.0 * sharpness - weight_old)
        direction = weight_new * weight_old * direction + 2.0 * weight_new / halfwidth * (
            inverse_diag * residual
        )
        solution = solution + direction
        residual = residual - apply_fn(direction)
        weight_old = weight_new
    return (solution, residual)


def pad_groups(array, starts):
    cont = jnp.where(starts[..., 1:] == 0, 1.0, 0.0)
    closed = jnp.zeros_like(cont[..., :1])
    lower = jnp.concatenate([closed, cont], axis=-1)[..., None, None, None]
    upper = jnp.concatenate([cont, closed], axis=-1)[..., None, None, None]
    below = (
        jnp.concatenate(
            [jnp.zeros_like(array[..., :1, :, :1, :]), array[..., :-1, :, -1:, :]], axis=-4
        )
        * lower
    )
    above = (
        jnp.concatenate(
            [array[..., 1:, :, :1, :], jnp.zeros_like(array[..., :1, :, :1, :])], axis=-4
        )
        * upper
    )
    joined = jnp.concatenate([below, array, above], axis=-2)
    widths = [(0, 0)] * (joined.ndim - 3) + [(1, 1), (0, 0), (1, 1)]
    return jnp.pad(joined, widths)


def same_group(starts):
    count = starts.shape[-1]
    marks = jnp.where(jnp.arange(count, dtype=jnp.int32) > 0, starts, 0)
    labels = jnp.cumsum(marks, axis=-1)
    return jnp.where(labels[..., :, None] == labels[..., None, :], 1.0, 0.0).astype(jnp.float32)


def shards(rhs_field, shear_modulus, lame_lambda, group_start):
    coefficients = jnp.stack([shear_modulus, lame_lambda])
    padded = padded_2(coefficients, (("gx", 1), ("gy", 2)), 1)
    padded = jnp.pad(padded, ((0, 0), (0, 0), (0, 0), (1, 1)))
    mu_pad = padded[0]
    lam_pad = padded[1]
    inverse_diag = 1.0 / diagonal(mu_pad, lam_pad, 1.0)

    def fine_apply(field):
        extended = padded_2(field, (("gx", 1), ("gy", 2)), 1)
        extended = jnp.pad(extended, ((0, 0), (0, 0), (0, 0), (1, 1)))
        return operate(extended, mu_pad, lam_pad, 1.0)

    solution, residual = smooth(
        jnp.zeros_like(rhs_field), rhs_field, inverse_diag, fine_apply, SWEEPS
    )
    coarse_x = rhs_field.shape[1] // 2
    coarse_y = rhs_field.shape[2] // 2
    coarse_z = rhs_field.shape[3] // 2
    coarse_res = residual.reshape(3, coarse_x, 2, coarse_y, 2, coarse_z, 2).sum(axis=(2, 4, 6))
    coarse_mu = shear_modulus.reshape(coarse_x, 2, coarse_y, 2, coarse_z, 2).mean(axis=(1, 3, 5))
    coarse_lam = lame_lambda.reshape(coarse_x, 2, coarse_y, 2, coarse_z, 2).mean(axis=(1, 3, 5))
    starts = group_start[0]
    position = lax.axis_index("gy")
    members = same_group(starts)
    my_members = lax.dynamic_index_in_dim(members, position, 0, keepdims=False)
    cells_dev = coarse_x * coarse_y * coarse_z
    group_cells = jnp.sum(my_members) * cells_dev
    packed = jnp.concatenate([coarse_res, jnp.stack([coarse_mu, coarse_lam])], axis=0)[:, None]
    column = lax.all_gather(packed, "gy", axis=1, tiled=True)
    coef_pad = pad_groups(column[3:5], starts)
    coarse_inverse = 1.0 / diagonal(coef_pad[0], coef_pad[1], 4.0)

    def coarse_apply(field):
        return operate(pad_groups(field, starts), coef_pad[0], coef_pad[1], 4.0)

    column_res = column[0:3]
    smoothed, coarse_left = smooth(
        jnp.zeros_like(column_res), column_res, coarse_inverse, coarse_apply, COARSE_SWEEPS
    )
    mine = lax.dynamic_index_in_dim(smoothed, position, 1, keepdims=False)
    device_sums = column_res.sum(axis=(2, 3, 4))
    totals = jnp.sum(device_sums * my_members[None, :], axis=1)
    group_shift = totals / (SHIFT_SCALE * group_cells)
    mine = mine + group_shift[:, None, None, None]
    fine_corr = jnp.broadcast_to(
        mine[:, :, None, :, None, :, None], (3, coarse_x, 2, coarse_y, 2, coarse_z, 2)
    ).reshape(rhs_field.shape)
    solution = solution + fine_corr
    residual = residual - fine_apply(fine_corr)
    solution, residual = smooth(solution, residual, inverse_diag, fine_apply, SWEEPS)
    return (solution, residual)


def solution(mesh):
    return jax.shard_map(
        shards,
        mesh=mesh,
        in_specs=(
            P(None, "gx", "gy", None),
            P("gx", "gy", None),
            P("gx", "gy", None),
            P("gx", None),
        ),
        out_specs=(P(None, "gx", "gy", None), P(None, "gx", "gy", None)),
        check_vma=False,
    )
```

profile of v0, /device:TPU:3, one launch (start us, length us, event | category | flops | bytes accessed | tf_op | source)
XLA Modules:
  0.0 176.6 jit_solution(6509398195644873209)
XLA Ops:
  1.5 3.7 %collective-permute-start = (f32[2,1,32,128]{3,2,1,0:T(8,128)S(1)}, f32[2,1,32,128]{3,2,1,0:T(8,128)S(1)}, u32[]{:S(2)}, u32[]{:S(2)}) collective-permute-start(f32[2,1,32,128]{3,2,1,0:T(8,128)S(1)} %get-tuple-element.123), channel_id=1, source_target_pairs={{0,4},{4,8},{8,12},{12,16},{16,20},{20,24},{24,28},{1,5},{5,9},{9,... | collective-permute-start | bytes 98312 | tf_op jit(solution)/shard_map/ppermute | solution.py:21
  7.1 4.2 %collective-permute-done.1 = f32[2,1,32,128]{3,2,1,0:T(8,128)S(1)} collective-permute-done((f32[2,1,32,128]{3,2,1,0:T(8,128)S(1)}, f32[2,1,32,128]{3,2,1,0:T(8,128)S(1)}, u32[]{:S(2)}, u32[]{:S(2)}) %collective-permute-start.1) | collective-permute-done | bytes 32800 | tf_op jit(solution)/shard_map/ppermute | solution.py:24
  12.0 3.2 %collective-permute-start.2 = (f32[2,4,1,128]{3,2,1,0:T(1,128)S(1)}, f32[2,4,1,128]{3,2,1,0:T(1,128)S(1)}, u32[]{:S(2)}, u32[]{:S(2)}) collective-permute-start(f32[2,4,1,128]{3,2,1,0:T(1,128)S(1)} %get-tuple-element.101), channel_id=1, source_target_pairs={{0,1},{1,2},{2,3},{4,5},{5,6},{6,7},{8,9},{9,10},{10,11},{12,13},{... | collective-permute-start | bytes 12296 | tf_op jit(solution)/shard_map/ppermute | solution.py:21
  20.9 3.3 %collective-permute-start.4 = (f32[3,1,32,128]{3,2,1,0:T(8,128)S(1)}, f32[3,1,32,128]{3,2,1,0:T(8,128)S(1)}, u32[]{:S(2)}, u32[]{:S(2)}) collective-permute-start(f32[3,1,32,128]{3,2,1,0:T(8,128)S(1)} %get-tuple-element.121), channel_id=1, source_target_pairs={{0,4},{4,8},{8,12},{12,16},{16,20},{20,24},{24,28},{1,5},{5,9},{9,... | collective-permute-start | bytes 147464 | tf_op jit(solution)/shard_map/ppermute | solution.py:21
  27.4 3.1 %collective-permute-done.5 = f32[3,1,32,128]{3,2,1,0:T(8,128)S(1)} collective-permute-done((f32[3,1,32,128]{3,2,1,0:T(8,128)S(1)}, f32[3,1,32,128]{3,2,1,0:T(8,128)S(1)}, u32[]{:S(2)}, u32[]{:S(2)}) %collective-permute-start.5) | collective-permute-done | bytes 49184 | tf_op jit(solution)/shard_map/ppermute | solution.py:24
  30.5 3.2 %collective-permute-start.6 = (f32[3,4,1,128]{3,2,1,0:T(1,128)S(1)}, f32[3,4,1,128]{3,2,1,0:T(1,128)S(1)}, u32[]{:S(2)}, u32[]{:S(2)}) collective-permute-start(f32[3,4,1,128]{3,2,1,0:T(1,128)S(1)} %get-tuple-element.93), channel_id=1, source_target_pairs={{0,1},{1,2},{2,3},{4,5},{5,6},{6,7},{8,9},{9,10},{10,11},{12,13},{... | collective-permute-start | bytes 18440 | tf_op jit(solution)/shard_map/ppermute | solution.py:21
  35.1 3.1 %collective-permute-done.7 = f32[3,4,1,128]{3,2,1,0:T(1,128)S(1)} collective-permute-done((f32[3,4,1,128]{3,2,1,0:T(1,128)S(1)}, f32[3,4,1,128]{3,2,1,0:T(1,128)S(1)}, u32[]{:S(2)}, u32[]{:S(2)}) %collective-permute-start.7) | collective-permute-done | bytes 6176 | tf_op jit(solution)/shard_map/ppermute | solution.py:24
  39.0 3.3 %collective-permute-start.8 = (f32[3,1,32,128]{3,2,1,0:T(8,128)S(1)}, f32[3,1,32,128]{3,2,1,0:T(8,128)S(1)}, u32[]{:S(2)}, u32[]{:S(2)}) collective-permute-start(f32[3,1,32,128]{3,2,1,0:T(8,128)S(1)} %get-tuple-element.119), channel_id=1, source_target_pairs={{0,4},{4,8},{8,12},{12,16},{16,20},{20,24},{24,28},{1,5},{5,9},{9,... | collective-permute-start | bytes 147464 | tf_op jit(solution)/shard_map/ppermute | solution.py:21
  44.5 4.2 %collective-permute-done.9 = f32[3,1,32,128]{3,2,1,0:T(8,128)S(1)} collective-permute-done((f32[3,1,32,128]{3,2,1,0:T(8,128)S(1)}, f32[3,1,32,128]{3,2,1,0:T(8,128)S(1)}, u32[]{:S(2)}, u32[]{:S(2)}) %collective-permute-start.9) | collective-permute-done | bytes 49184 | tf_op jit(solution)/shard_map/ppermute | solution.py:24
  48.7 3.2 %collective-permute-start.10 = (f32[3,4,1,128]{3,2,1,0:T(1,128)S(1)}, f32[3,4,1,128]{3,2,1,0:T(1,128)S(1)}, u32[]{:S(2)}, u32[]{:S(2)}) collective-permute-start(f32[3,4,1,128]{3,2,1,0:T(1,128)S(1)} %get-tuple-element.91), channel_id=1, source_target_pairs={{0,1},{1,2},{2,3},{4,5},{5,6},{6,7},{8,9},{9,10},{10,11},{12,13},{... | collective-permute-start | bytes 18440 | tf_op jit(solution)/shard_map/ppermute | solution.py:21
  53.3 3.0 %collective-permute-done.11 = f32[3,4,1,128]{3,2,1,0:T(1,128)S(1)} collective-permute-done((f32[3,4,1,128]{3,2,1,0:T(1,128)S(1)}, f32[3,4,1,128]{3,2,1,0:T(1,128)S(1)}, u32[]{:S(2)}, u32[]{:S(2)}) %collective-permute-start.11) | collective-permute-done | bytes 6176 | tf_op jit(solution)/shard_map/ppermute | solution.py:24
  57.2 3.3 %collective-permute-start.12 = (f32[3,1,32,128]{3,2,1,0:T(8,128)S(1)}, f32[3,1,32,128]{3,2,1,0:T(8,128)S(1)}, u32[]{:S(2)}, u32[]{:S(2)}) collective-permute-start(f32[3,1,32,128]{3,2,1,0:T(8,128)S(1)} %get-tuple-element.117), channel_id=1, source_target_pairs={{0,4},{4,8},{8,12},{12,16},{16,20},{20,24},{24,28},{1,5},{5,9},{9,... | collective-permute-start | bytes 147464 | tf_op jit(solution)/shard_map/ppermute | solution.py:21
  62.5 4.3 %collective-permute-done.13 = f32[3,1,32,128]{3,2,1,0:T(8,128)S(1)} collective-permute-done((f32[3,1,32,128]{3,2,1,0:T(8,128)S(1)}, f32[3,1,32,128]{3,2,1,0:T(8,128)S(1)}, u32[]{:S(2)}, u32[]{:S(2)}) %collective-permute-start.13) | collective-permute-done | bytes 49184 | tf_op jit(solution)/shard_map/ppermute | solution.py:24
  66.9 2.1 %collective-permute-start.14 = (f32[3,4,1,128]{3,2,1,0:T(1,128)S(1)}, f32[3,4,1,128]{3,2,1,0:T(1,128)S(1)}, u32[]{:S(2)}, u32[]{:S(2)}) collective-permute-start(f32[3,4,1,128]{3,2,1,0:T(1,128)S(1)} %get-tuple-element.89), channel_id=1, source_target_pairs={{0,1},{1,2},{2,3},{4,5},{5,6},{6,7},{8,9},{9,10},{10,11},{12,13},{... | collective-permute-start | bytes 18440 | tf_op jit(solution)/shard_map/ppermute | solution.py:21
  75.4 3.9 %reduce_sum.62 = f32[3,16,2,64,2]{4,3,2,1,0:T(8,128)S(1)} reshape(f32[3,32,128]{2,1,0:T(8,128)} %fusion.450) | data formatting | bytes 98304 | tf_op jit(solution)/shard_map/reduce_sum | solution.py:161
  81.1 11.4 %all-gather = f32[5,4,16,64]{3,2,1,0:T(8,128)S(1)} all-gather(f32[5,1,16,64]{3,2,1,0:T(8,128)S(1)} %pad_maximum_fusion), channel_id=2, replica_groups=mesh['gx'=8,'gy'=4] {'gy'}, dimensions={1}, use_global_device_ids=true | all-gather | bytes 102400 | tf_op jit(solution)/shard_map/all_gather | solution.py:171
  99.3 2.7 %slice.1640 = f32[3,1,32,128]{3,2,0,1:T(8,128)} reshape(f32[3,16,2,64,2]{4,3,2,1,0:T(8,128)S(1)} %broadcast_in_dim.46) | data formatting | bytes 98304 | tf_op jit(solution)/shard_map/slice | solution.py:22
  102.0 2.6 %collective-permute-start.17 = (f32[3,1,32,128]{3,2,0,1:T(8,128)}, f32[3,1,32,128]{3,2,0,1:T(8,128)}, u32[]{:S(2)}, u32[]{:S(2)}) collective-permute-start(f32[3,1,32,128]{3,2,0,1:T(8,128)} %slice.1640), channel_id=1, source_target_pairs={{4,0},{8,4},{12,8},{16,12},{20,16},{24,20},{28,24},{5,1},{9,5},{13... | collective-permute-start | bytes 147464 | tf_op jit(solution)/shard_map/ppermute | solution.py:24
  104.6 4.9 %collective-permute-start.16 = (f32[3,1,32,128]{3,2,0,1:T(8,128)}, f32[3,1,32,128]{3,2,0,1:T(8,128)}, u32[]{:S(2)}, u32[]{:S(2)}) collective-permute-start(f32[3,1,32,128]{3,2,0,1:T(8,128)} %slice.1640), channel_id=1, source_target_pairs={{0,4},{4,8},{8,12},{12,16},{16,20},{20,24},{24,28},{1,5},{5,9},{9,... | collective-permute-start | bytes 147464 | tf_op jit(solution)/shard_map/ppermute | solution.py:21
  109.4 2.7 %broadcast_in_dim.47 = f32[3,32,128]{2,1,0:T(8,128)} reshape(f32[3,16,2,64,2]{4,3,2,1,0:T(8,128)S(1)} %broadcast_in_dim.46) | data formatting | bytes 98304 | tf_op jit(solution)/shard_map/broadcast_in_dim | solution.py:187
  116.5 3.1 %collective-permute-done.19 = f32[3,4,1,128]{3,2,1,0:T(1,128)S(1)} collective-permute-done((f32[3,4,1,128]{3,2,1,0:T(1,128)S(1)}, f32[3,4,1,128]{3,2,1,0:T(1,128)S(1)}, u32[]{:S(2)}, u32[]{:S(2)}) %collective-permute-start.19) | collective-permute-done | bytes 6176 | tf_op jit(solution)/shard_map/ppermute | solution.py:24
  121.3 4.9 %collective-permute-start.20 = (f32[3,1,32,128]{3,2,1,0:T(8,128)S(1)}, f32[3,1,32,128]{3,2,1,0:T(8,128)S(1)}, u32[]{:S(2)}, u32[]{:S(2)}) collective-permute-start(f32[3,1,32,128]{3,2,1,0:T(8,128)S(1)} %get-tuple-element.107), channel_id=1, source_target_pairs={{0,4},{4,8},{8,12},{12,16},{16,20},{20,24},{24,28},{1,5},{5,9},{9,... | collective-permute-start | bytes 147464 | tf_op jit(solution)/shard_map/ppermute | solution.py:21
  128.2 4.4 %collective-permute-done.21 = f32[3,1,32,128]{3,2,1,0:T(8,128)S(1)} collective-permute-done((f32[3,1,32,128]{3,2,1,0:T(8,128)S(1)}, f32[3,1,32,128]{3,2,1,0:T(8,128)S(1)}, u32[]{:S(2)}, u32[]{:S(2)}) %collective-permute-start.21) | collective-permute-done | bytes 49184 | tf_op jit(solution)/shard_map/ppermute | solution.py:24
  132.5 3.4 %collective-permute-start.22 = (f32[3,4,1,128]{3,2,1,0:T(1,128)S(1)}, f32[3,4,1,128]{3,2,1,0:T(1,128)S(1)}, u32[]{:S(2)}, u32[]{:S(2)}) collective-permute-start(f32[3,4,1,128]{3,2,1,0:T(1,128)S(1)} %get-tuple-element.85), channel_id=1, source_target_pairs={{0,1},{1,2},{2,3},{4,5},{5,6},{6,7},{8,9},{9,10},{10,11},{12,13},{... | collective-permute-start | bytes 18440 | tf_op jit(solution)/shard_map/ppermute | solution.py:21
  137.3 3.1 %collective-permute-done.23 = f32[3,4,1,128]{3,2,1,0:T(1,128)S(1)} collective-permute-done((f32[3,4,1,128]{3,2,1,0:T(1,128)S(1)}, f32[3,4,1,128]{3,2,1,0:T(1,128)S(1)}, u32[]{:S(2)}, u32[]{:S(2)}) %collective-permute-start.23) | collective-permute-done | bytes 6176 | tf_op jit(solution)/shard_map/ppermute | solution.py:24
  141.3 3.3 %collective-permute-start.24 = (f32[3,1,32,128]{3,2,1,0:T(8,128)S(1)}, f32[3,1,32,128]{3,2,1,0:T(8,128)S(1)}, u32[]{:S(2)}, u32[]{:S(2)}) collective-permute-start(f32[3,1,32,128]{3,2,1,0:T(8,128)S(1)} %get-tuple-element.105), channel_id=1, source_target_pairs={{0,4},{4,8},{8,12},{12,16},{16,20},{20,24},{24,28},{1,5},{5,9},{9,... | collective-permute-start | bytes 147464 | tf_op jit(solution)/shard_map/ppermute | solution.py:21
  146.6 4.4 %collective-permute-done.25 = f32[3,1,32,128]{3,2,1,0:T(8,128)S(1)} collective-permute-done((f32[3,1,32,128]{3,2,1,0:T(8,128)S(1)}, f32[3,1,32,128]{3,2,1,0:T(8,128)S(1)}, u32[]{:S(2)}, u32[]{:S(2)}) %collective-permute-start.25) | collective-permute-done | bytes 49184 | tf_op jit(solution)/shard_map/ppermute | solution.py:24
  150.9 2.5 %collective-permute-start.26 = (f32[3,4,1,128]{3,2,1,0:T(1,128)S(1)}, f32[3,4,1,128]{3,2,1,0:T(1,128)S(1)}, u32[]{:S(2)}, u32[]{:S(2)}) collective-permute-start(f32[3,4,1,128]{3,2,1,0:T(1,128)S(1)} %get-tuple-element.83), channel_id=1, source_target_pairs={{0,1},{1,2},{2,3},{4,5},{5,6},{6,7},{8,9},{9,10},{10,11},{12,13},{... | collective-permute-start | bytes 18440 | tf_op jit(solution)/shard_map/ppermute | solution.py:21
  154.7 3.1 %collective-permute-done.27 = f32[3,4,1,128]{3,2,1,0:T(1,128)S(1)} collective-permute-done((f32[3,4,1,128]{3,2,1,0:T(1,128)S(1)}, f32[3,4,1,128]{3,2,1,0:T(1,128)S(1)}, u32[]{:S(2)}, u32[]{:S(2)}) %collective-permute-start.27) | collective-permute-done | bytes 6176 | tf_op jit(solution)/shard_map/ppermute | solution.py:24
  159.4 3.3 %collective-permute-start.28 = (f32[3,1,32,128]{3,2,1,0:T(8,128)S(1)}, f32[3,1,32,128]{3,2,1,0:T(8,128)S(1)}, u32[]{:S(2)}, u32[]{:S(2)}) collective-permute-start(f32[3,1,32,128]{3,2,1,0:T(8,128)S(1)} %get-tuple-element.103), channel_id=1, source_target_pairs={{0,4},{4,8},{8,12},{12,16},{16,20},{20,24},{24,28},{1,5},{5,9},{9,... | collective-permute-start | bytes 147464 | tf_op jit(solution)/shard_map/ppermute | solution.py:21
  164.7 4.4 %collective-permute-done.29 = f32[3,1,32,128]{3,2,1,0:T(8,128)S(1)} collective-permute-done((f32[3,1,32,128]{3,2,1,0:T(8,128)S(1)}, f32[3,1,32,128]{3,2,1,0:T(8,128)S(1)}, u32[]{:S(2)}, u32[]{:S(2)}) %collective-permute-start.29) | collective-permute-done | bytes 49184 | tf_op jit(solution)/shard_map/ppermute | solution.py:24
  172.0 3.1 %collective-permute-done.31 = f32[3,4,1,128]{3,2,1,0:T(1,128)S(1)} collective-permute-done((f32[3,4,1,128]{3,2,1,0:T(1,128)S(1)}, f32[3,4,1,128]{3,2,1,0:T(1,128)S(1)}, u32[]{:S(2)}, u32[]{:S(2)}) %collective-permute-start.31) | collective-permute-done | bytes 6176 | tf_op jit(solution)/shard_map/ppermute | solution.py:24
  (213 shorter events, 55.9 us)
Async XLA Ops:
  1.5 5.6 %collective-permute-start = (f32[2,1,32,128]{3,2,1,0:T(8,128)S(1)}, f32[2,1,32,128]{3,2,1,0:T(8,128)S(1)}, u32[]{:S(2)}, u32[]{:S(2)}) collective-permute-start(f32[2,1,32,128]{3,2,1,0:T(8,128)S(1)} %get-tuple-element.123), channel_id=1, source_target_pairs={{0,4},{4,8},{8,12},{12,16},{16,20},{20,24},{24,28},{1,5},{5,9},{9,... | collective-permute-start | bytes 98312 | tf_op jit(solution)/shard_map/ppermute | solution.py:21
  5.1 6.1 %collective-permute-start.1 = (f32[2,1,32,128]{3,2,1,0:T(8,128)S(1)}, f32[2,1,32,128]{3,2,1,0:T(8,128)S(1)}, u32[]{:S(2)}, u32[]{:S(2)}) collective-permute-start(f32[2,1,32,128]{3,2,1,0:T(8,128)S(1)} %get-tuple-element.124), channel_id=1, source_target_pairs={{4,0},{8,4},{12,8},{16,12},{20,16},{24,20},{28,24},{5,1},{9,5},{13... | collective-permute-start | bytes 98312 | tf_op jit(solution)/shard_map/ppermute | solution.py:24
  12.0 6.5 %collective-permute-start.2 = (f32[2,4,1,128]{3,2,1,0:T(1,128)S(1)}, f32[2,4,1,128]{3,2,1,0:T(1,128)S(1)}, u32[]{:S(2)}, u32[]{:S(2)}) collective-permute-start(f32[2,4,1,128]{3,2,1,0:T(1,128)S(1)} %get-tuple-element.101), channel_id=1, source_target_pairs={{0,1},{1,2},{2,3},{4,5},{5,6},{6,7},{8,9},{9,10},{10,11},{12,13},{... | collective-permute-start | bytes 12296 | tf_op jit(solution)/shard_map/ppermute | solution.py:21
  15.2 4.4 %collective-permute-start.3 = (f32[2,4,1,128]{3,2,1,0:T(1,128)S(1)}, f32[2,4,1,128]{3,2,1,0:T(1,128)S(1)}, u32[]{:S(2)}, u32[]{:S(2)}) collective-permute-start(f32[2,4,1,128]{3,2,1,0:T(1,128)S(1)} %get-tuple-element.102), channel_id=1, source_target_pairs={{1,0},{2,1},{3,2},{5,4},{6,5},{7,6},{9,8},{10,9},{11,10},{13,12},{... | collective-permute-start | bytes 12296 | tf_op jit(solution)/shard_map/ppermute | solution.py:24
  20.9 6.6 %collective-permute-start.4 = (f32[3,1,32,128]{3,2,1,0:T(8,128)S(1)}, f32[3,1,32,128]{3,2,1,0:T(8,128)S(1)}, u32[]{:S(2)}, u32[]{:S(2)}) collective-permute-start(f32[3,1,32,128]{3,2,1,0:T(8,128)S(1)} %get-tuple-element.121), channel_id=1, source_target_pairs={{0,4},{4,8},{8,12},{12,16},{16,20},{20,24},{24,28},{1,5},{5,9},{9,... | collective-permute-start | bytes 147464 | tf_op jit(solution)/shard_map/ppermute | solution.py:21
  24.2 6.3 %collective-permute-start.5 = (f32[3,1,32,128]{3,2,1,0:T(8,128)S(1)}, f32[3,1,32,128]{3,2,1,0:T(8,128)S(1)}, u32[]{:S(2)}, u32[]{:S(2)}) collective-permute-start(f32[3,1,32,128]{3,2,1,0:T(8,128)S(1)} %get-tuple-element.122), channel_id=1, source_target_pairs={{4,0},{8,4},{12,8},{16,12},{20,16},{24,20},{28,24},{5,1},{9,5},{13... | collective-permute-start | bytes 147464 | tf_op jit(solution)/shard_map/ppermute | solution.py:24
  30.5 4.5 %collective-permute-start.6 = (f32[3,4,1,128]{3,2,1,0:T(1,128)S(1)}, f32[3,4,1,128]{3,2,1,0:T(1,128)S(1)}, u32[]{:S(2)}, u32[]{:S(2)}) collective-permute-start(f32[3,4,1,128]{3,2,1,0:T(1,128)S(1)} %get-tuple-element.93), channel_id=1, source_target_pairs={{0,1},{1,2},{2,3},{4,5},{5,6},{6,7},{8,9},{9,10},{10,11},{12,13},{... | collective-permute-start | bytes 18440 | tf_op jit(solution)/shard_map/ppermute | solution.py:21
  33.7 4.4 %collective-permute-start.7 = (f32[3,4,1,128]{3,2,1,0:T(1,128)S(1)}, f32[3,4,1,128]{3,2,1,0:T(1,128)S(1)}, u32[]{:S(2)}, u32[]{:S(2)}) collective-permute-start(f32[3,4,1,128]{3,2,1,0:T(1,128)S(1)} %get-tuple-element.94), channel_id=1, source_target_pairs={{1,0},{2,1},{3,2},{5,4},{6,5},{7,6},{9,8},{10,9},{11,10},{13,12},{... | collective-permute-start | bytes 18440 | tf_op jit(solution)/shard_map/ppermute | solution.py:24
  39.0 5.5 %collective-permute-start.8 = (f32[3,1,32,128]{3,2,1,0:T(8,128)S(1)}, f32[3,1,32,128]{3,2,1,0:T(8,128)S(1)}, u32[]{:S(2)}, u32[]{:S(2)}) collective-permute-start(f32[3,1,32,128]{3,2,1,0:T(8,128)S(1)} %get-tuple-element.119), channel_id=1, source_target_pairs={{0,4},{4,8},{8,12},{12,16},{16,20},{20,24},{24,28},{1,5},{5,9},{9,... | collective-permute-start | bytes 147464 | tf_op jit(solution)/shard_map/ppermute | solution.py:21
  42.4 6.3 %collective-permute-start.9 = (f32[3,1,32,128]{3,2,1,0:T(8,128)S(1)}, f32[3,1,32,128]{3,2,1,0:T(8,128)S(1)}, u32[]{:S(2)}, u32[]{:S(2)}) collective-permute-start(f32[3,1,32,128]{3,2,1,0:T(8,128)S(1)} %get-tuple-element.120), channel_id=1, source_target_pairs={{4,0},{8,4},{12,8},{16,12},{20,16},{24,20},{28,24},{5,1},{9,5},{13... | collective-permute-start | bytes 147464 | tf_op jit(solution)/shard_map/ppermute | solution.py:24
  48.7 4.6 %collective-permute-start.10 = (f32[3,4,1,128]{3,2,1,0:T(1,128)S(1)}, f32[3,4,1,128]{3,2,1,0:T(1,128)S(1)}, u32[]{:S(2)}, u32[]{:S(2)}) collective-permute-start(f32[3,4,1,128]{3,2,1,0:T(1,128)S(1)} %get-tuple-element.91), channel_id=1, source_target_pairs={{0,1},{1,2},{2,3},{4,5},{5,6},{6,7},{8,9},{9,10},{10,11},{12,13},{... | collective-permute-start | bytes 18440 | tf_op jit(solution)/shard_map/ppermute | solution.py:21
  51.9 4.4 %collective-permute-start.11 = (f32[3,4,1,128]{3,2,1,0:T(1,128)S(1)}, f32[3,4,1,128]{3,2,1,0:T(1,128)S(1)}, u32[]{:S(2)}, u32[]{:S(2)}) collective-permute-start(f32[3,4,1,128]{3,2,1,0:T(1,128)S(1)} %get-tuple-element.92), channel_id=1, source_target_pairs={{1,0},{2,1},{3,2},{5,4},{6,5},{7,6},{9,8},{10,9},{11,10},{13,12},{... | collective-permute-start | bytes 18440 | tf_op jit(solution)/shard_map/ppermute | solution.py:24
  57.2 5.3 %collective-permute-start.12 = (f32[3,1,32,128]{3,2,1,0:T(8,128)S(1)}, f32[3,1,32,128]{3,2,1,0:T(8,128)S(1)}, u32[]{:S(2)}, u32[]{:S(2)}) collective-permute-start(f32[3,1,32,128]{3,2,1,0:T(8,128)S(1)} %get-tuple-element.117), channel_id=1, source_target_pairs={{0,4},{4,8},{8,12},{12,16},{16,20},{20,24},{24,28},{1,5},{5,9},{9,... | collective-permute-start | bytes 147464 | tf_op jit(solution)/shard_map/ppermute | solution.py:21
  60.5 6.3 %collective-permute-start.13 = (f32[3,1,32,128]{3,2,1,0:T(8,128)S(1)}, f32[3,1,32,128]{3,2,1,0:T(8,128)S(1)}, u32[]{:S(2)}, u32[]{:S(2)}) collective-permute-start(f32[3,1,32,128]{3,2,1,0:T(8,128)S(1)} %get-tuple-element.118), channel_id=1, source_target_pairs={{4,0},{8,4},{12,8},{16,12},{20,16},{24,20},{28,24},{5,1},{9,5},{13... | collective-permute-start | bytes 147464 | tf_op jit(solution)/shard_map/ppermute | solution.py:24
  66.9 5.8 %collective-permute-start.14 = (f32[3,4,1,128]{3,2,1,0:T(1,128)S(1)}, f32[3,4,1,128]{3,2,1,0:T(1,128)S(1)}, u32[]{:S(2)}, u32[]{:S(2)}) collective-permute-start(f32[3,4,1,128]{3,2,1,0:T(1,128)S(1)} %get-tuple-element.89), channel_id=1, source_target_pairs={{0,1},{1,2},{2,3},{4,5},{5,6},{6,7},{8,9},{9,10},{10,11},{12,13},{... | collective-permute-start | bytes 18440 | tf_op jit(solution)/shard_map/ppermute | solution.py:21
  69.0 4.4 %collective-permute-start.15 = (f32[3,4,1,128]{3,2,1,0:T(1,128)S(1)}, f32[3,4,1,128]{3,2,1,0:T(1,128)S(1)}, u32[]{:S(2)}, u32[]{:S(2)}) collective-permute-start(f32[3,4,1,128]{3,2,1,0:T(1,128)S(1)} %get-tuple-element.90), channel_id=1, source_target_pairs={{1,0},{2,1},{3,2},{5,4},{6,5},{7,6},{9,8},{10,9},{11,10},{13,12},{... | collective-permute-start | bytes 18440 | tf_op jit(solution)/shard_map/ppermute | solution.py:24
  102.0 10.2 %collective-permute-start.17 = (f32[3,1,32,128]{3,2,0,1:T(8,128)}, f32[3,1,32,128]{3,2,0,1:T(8,128)}, u32[]{:S(2)}, u32[]{:S(2)}) collective-permute-start(f32[3,1,32,128]{3,2,0,1:T(8,128)} %slice.1640), channel_id=1, source_target_pairs={{4,0},{8,4},{12,8},{16,12},{20,16},{24,20},{28,24},{5,1},{9,5},{13... | collective-permute-start | bytes 147464 | tf_op jit(solution)/shard_map/ppermute | solution.py:24
  104.6 7.6 %collective-permute-start.16 = (f32[3,1,32,128]{3,2,0,1:T(8,128)}, f32[3,1,32,128]{3,2,0,1:T(8,128)}, u32[]{:S(2)}, u32[]{:S(2)}) collective-permute-start(f32[3,1,32,128]{3,2,0,1:T(8,128)} %slice.1640), channel_id=1, source_target_pairs={{0,4},{4,8},{8,12},{12,16},{16,20},{20,24},{24,28},{1,5},{5,9},{9,... | collective-permute-start | bytes 147464 | tf_op jit(solution)/shard_map/ppermute | solution.py:21
  113.9 2.6 %collective-permute-start.18 = (f32[3,4,1,128]{3,2,1,0:T(1,128)S(1)}, f32[3,4,1,128]{3,2,1,0:T(1,128)S(1)}, u32[]{:S(2)}, u32[]{:S(2)}) collective-permute-start(f32[3,4,1,128]{3,2,1,0:T(1,128)S(1)} %get-tuple-element.87), channel_id=1, source_target_pairs={{0,1},{1,2},{2,3},{4,5},{5,6},{6,7},{8,9},{9,10},{10,11},{12,13},{... | collective-permute-start | bytes 18440 | tf_op jit(solution)/shard_map/ppermute | solution.py:21
  115.1 4.4 %collective-permute-start.19 = (f32[3,4,1,128]{3,2,1,0:T(1,128)S(1)}, f32[3,4,1,128]{3,2,1,0:T(1,128)S(1)}, u32[]{:S(2)}, u32[]{:S(2)}) collective-permute-start(f32[3,4,1,128]{3,2,1,0:T(1,128)S(1)} %get-tuple-element.88), channel_id=1, source_target_pairs={{1,0},{2,1},{3,2},{5,4},{6,5},{7,6},{9,8},{10,9},{11,10},{13,12},{... | collective-permute-start | bytes 18440 | tf_op jit(solution)/shard_map/ppermute | solution.py:24
  121.3 6.9 %collective-permute-start.20 = (f32[3,1,32,128]{3,2,1,0:T(8,128)S(1)}, f32[3,1,32,128]{3,2,1,0:T(8,128)S(1)}, u32[]{:S(2)}, u32[]{:S(2)}) collective-permute-start(f32[3,1,32,128]{3,2,1,0:T(8,128)S(1)} %get-tuple-element.107), channel_id=1, source_target_pairs={{0,4},{4,8},{8,12},{12,16},{16,20},{20,24},{24,28},{1,5},{5,9},{9,... | collective-permute-start | bytes 147464 | tf_op jit(solution)/shard_map/ppermute | solution.py:21
  126.2 6.3 %collective-permute-start.21 = (f32[3,1,32,128]{3,2,1,0:T(8,128)S(1)}, f32[3,1,32,128]{3,2,1,0:T(8,128)S(1)}, u32[]{:S(2)}, u32[]{:S(2)}) collective-permute-start(f32[3,1,32,128]{3,2,1,0:T(8,128)S(1)} %get-tuple-element.108), channel_id=1, source_target_pairs={{4,0},{8,4},{12,8},{16,12},{20,16},{24,20},{28,24},{5,1},{9,5},{13... | collective-permute-start | bytes 147464 | tf_op jit(solution)/shard_map/ppermute | solution.py:24
  132.5 4.7 %collective-permute-start.22 = (f32[3,4,1,128]{3,2,1,0:T(1,128)S(1)}, f32[3,4,1,128]{3,2,1,0:T(1,128)S(1)}, u32[]{:S(2)}, u32[]{:S(2)}) collective-permute-start(f32[3,4,1,128]{3,2,1,0:T(1,128)S(1)} %get-tuple-element.85), channel_id=1, source_target_pairs={{0,1},{1,2},{2,3},{4,5},{5,6},{6,7},{8,9},{9,10},{10,11},{12,13},{... | collective-permute-start | bytes 18440 | tf_op jit(solution)/shard_map/ppermute | solution.py:21
  136.0 4.4 %collective-permute-start.23 = (f32[3,4,1,128]{3,2,1,0:T(1,128)S(1)}, f32[3,4,1,128]{3,2,1,0:T(1,128)S(1)}, u32[]{:S(2)}, u32[]{:S(2)}) collective-permute-start(f32[3,4,1,128]{3,2,1,0:T(1,128)S(1)} %get-tuple-element.86), channel_id=1, source_target_pairs={{1,0},{2,1},{3,2},{5,4},{6,5},{7,6},{9,8},{10,9},{11,10},{13,12},{... | collective-permute-start | bytes 18440 | tf_op jit(solution)/shard_map/ppermute | solution.py:24
  141.3 5.3 %collective-permute-start.24 = (f32[3,1,32,128]{3,2,1,0:T(8,128)S(1)}, f32[3,1,32,128]{3,2,1,0:T(8,128)S(1)}, u32[]{:S(2)}, u32[]{:S(2)}) collective-permute-start(f32[3,1,32,128]{3,2,1,0:T(8,128)S(1)} %get-tuple-element.105), channel_id=1, source_target_pairs={{0,4},{4,8},{8,12},{12,16},{16,20},{20,24},{24,28},{1,5},{5,9},{9,... | collective-permute-start | bytes 147464 | tf_op jit(solution)/shard_map/ppermute | solution.py:21
  144.6 6.3 %collective-permute-start.25 = (f32[3,1,32,128]{3,2,1,0:T(8,128)S(1)}, f32[3,1,32,128]{3,2,1,0:T(8,128)S(1)}, u32[]{:S(2)}, u32[]{:S(2)}) collective-permute-start(f32[3,1,32,128]{3,2,1,0:T(8,128)S(1)} %get-tuple-element.106), channel_id=1, source_target_pairs={{4,0},{8,4},{12,8},{16,12},{20,16},{24,20},{28,24},{5,1},{9,5},{13... | collective-permute-start | bytes 147464 | tf_op jit(solution)/shard_map/ppermute | solution.py:24
  150.9 3.8 %collective-permute-start.26 = (f32[3,4,1,128]{3,2,1,0:T(1,128)S(1)}, f32[3,4,1,128]{3,2,1,0:T(1,128)S(1)}, u32[]{:S(2)}, u32[]{:S(2)}) collective-permute-start(f32[3,4,1,128]{3,2,1,0:T(1,128)S(1)} %get-tuple-element.83), channel_id=1, source_target_pairs={{0,1},{1,2},{2,3},{4,5},{5,6},{6,7},{8,9},{9,10},{10,11},{12,13},{... | collective-permute-start | bytes 18440 | tf_op jit(solution)/shard_map/ppermute | solution.py:21
  153.4 4.4 %collective-permute-start.27 = (f32[3,4,1,128]{3,2,1,0:T(1,128)S(1)}, f32[3,4,1,128]{3,2,1,0:T(1,128)S(1)}, u32[]{:S(2)}, u32[]{:S(2)}) collective-permute-start(f32[3,4,1,128]{3,2,1,0:T(1,128)S(1)} %get-tuple-element.84), channel_id=1, source_target_pairs={{1,0},{2,1},{3,2},{5,4},{6,5},{7,6},{9,8},{10,9},{11,10},{13,12},{... | collective-permute-start | bytes 18440 | tf_op jit(solution)/shard_map/ppermute | solution.py:24
  159.4 5.3 %collective-permute-start.28 = (f32[3,1,32,128]{3,2,1,0:T(8,128)S(1)}, f32[3,1,32,128]{3,2,1,0:T(8,128)S(1)}, u32[]{:S(2)}, u32[]{:S(2)}) collective-permute-start(f32[3,1,32,128]{3,2,1,0:T(8,128)S(1)} %get-tuple-element.103), channel_id=1, source_target_pairs={{0,4},{4,8},{8,12},{12,16},{16,20},{20,24},{24,28},{1,5},{5,9},{9,... | collective-permute-start | bytes 147464 | tf_op jit(solution)/shard_map/ppermute | solution.py:21
  162.7 6.3 %collective-permute-start.29 = (f32[3,1,32,128]{3,2,1,0:T(8,128)S(1)}, f32[3,1,32,128]{3,2,1,0:T(8,128)S(1)}, u32[]{:S(2)}, u32[]{:S(2)}) collective-permute-start(f32[3,1,32,128]{3,2,1,0:T(8,128)S(1)} %get-tuple-element.104), channel_id=1, source_target_pairs={{4,0},{8,4},{12,8},{16,12},{20,16},{24,20},{28,24},{5,1},{9,5},{13... | collective-permute-start | bytes 147464 | tf_op jit(solution)/shard_map/ppermute | solution.py:24
  169.1 3.0 %collective-permute-start.30 = (f32[3,4,1,128]{3,2,1,0:T(1,128)S(1)}, f32[3,4,1,128]{3,2,1,0:T(1,128)S(1)}, u32[]{:S(2)}, u32[]{:S(2)}) collective-permute-start(f32[3,4,1,128]{3,2,1,0:T(1,128)S(1)} %get-tuple-element.81), channel_id=1, source_target_pairs={{0,1},{1,2},{2,3},{4,5},{5,6},{6,7},{8,9},{9,10},{10,11},{12,13},{... | collective-permute-start | bytes 18440 | tf_op jit(solution)/shard_map/ppermute | solution.py:21
  170.7 4.4 %collective-permute-start.31 = (f32[3,4,1,128]{3,2,1,0:T(1,128)S(1)}, f32[3,4,1,128]{3,2,1,0:T(1,128)S(1)}, u32[]{:S(2)}, u32[]{:S(2)}) collective-permute-start(f32[3,4,1,128]{3,2,1,0:T(1,128)S(1)} %get-tuple-element.82), channel_id=1, source_target_pairs={{1,0},{2,1},{3,2},{5,4},{6,5},{7,6},{9,8},{10,9},{11,10},{13,12},{... | collective-permute-start | bytes 18440 | tf_op jit(solution)/shard_map/ppermute | solution.py:24
  (28 other events, 423.4 us)
where the time goes:
time: 178 us; the launch traced here: 177 us
  starting transfers between devices  76.9 us (43%)
  waiting for transfers between devices  49 us (28%)
  other arithmetic  22.8 us (13%)
  local copies, waits for them, and re-layouts  13.9 us (8%)
  blocking collectives  11.4 us (6%)
  between operations  2.56 us (1%)
    ppermute x16, starting transfers between devices, padded_2(): lax.ppermute(lax.slice_in_dim(block, block.shape[dim] - width, None, axis...  50.6 us
    ppermute x16, waiting for transfers between devices, padded_2(): lax.ppermute(lax.slice_in_dim(block, 0, width, axis=dim), axis, backward)  48.9 us
    ppermute x16, starting transfers between devices, padded_2(): lax.ppermute(lax.slice_in_dim(block, 0, width, axis=dim), axis, backward)  26.4 us
    all_gather x1, blocking collectives, shards(): column = lax.all_gather(packed, 'gy', axis=1, tiled=True)  11.4 us
    another operation x30, other arithmetic, operate(): return jnp.stack(results)  4.99 us
    broadcast_in_dim x3, local copies, waits for them, and re-layouts, shards(): jnp.broadcast_to(mine[:, :, None, :, None, :, None], (3, coarse_x, 2, coa...  4.06 us
    reduce_sum x1, local copies, waits for them, and re-layouts, shards(): residual.reshape(3, coarse_x, 2, coarse_y, 2, coarse_z, 2)  3.89 us
  transfers between devices with their start and end apart: 32, of which 15 were waited for; matrix products, arithmetic and copies ran while one was open for 5% of the time, Pallas kernels for 0%

commit v1 on v0

v1 whole, which is shorter than its diff:
```python
import functools

import jax
import jax.numpy as jnp
from jax import lax
from jax.experimental import pallas as pl
from jax.experimental.pallas import tpu as pltpu
from jax.sharding import PartitionSpec as P

SWEEPS = 3
COARSE_SWEEPS = 4
LOW_BOUND = 0.5
HIGH_BOUND = 6.0
SHIFT_SCALE = 48.0

MID = 0.5 * (HIGH_BOUND + LOW_BOUND)
HALF = 0.5 * (HIGH_BOUND - LOW_BOUND)
SIGMA = MID / HALF

H = 8
DIRS = ((1, 0), (-1, 0), (0, 1), (0, -1), (1, -1), (-1, 1), (1, 1), (-1, -1))


def weights(steps):
    out = [(0.0, 1.0 / MID)]
    old = 1.0 / SIGMA
    for _ in range(steps - 1):
        new = 1.0 / (2.0 * SIGMA - old)
        out.append((new * old, 2.0 * new / HALF))
        old = new
    return out


def kernel(
    n_gx, n_gy, rhs_ref, mu_ref, lam_ref, starts_ref, sol_ref, res_ref,
    coef, rhs, inv, dirs, rbuf, r2buf, fc, sums, send, recv, sum_send, sum_recv,
):
    rows = rhs_ref.shape[2]
    lanes = rhs_ref.shape[3]
    ext = rows + 2 * H
    gx = lax.axis_index("gx")
    gy = lax.axis_index("gy")
    own = slice(H, H + rows)

    def exists(sx, sy):
        ok = None
        for pos, step, count in ((gx, sx, n_gx), (gy, sy, n_gy)):
            if step == 1:
                here = pos < count - 1
            elif step == -1:
                here = pos > 0
            else:
                continue
            ok = here if ok is None else jnp.logical_and(ok, here)
        return ok

    coef[0, 2:4, own, :] = mu_ref[...]
    coef[1, 2:4, own, :] = lam_ref[...]
    rhs[:, 1:3, own, :] = rhs_ref[...]

    def clear(ref, index):
        ref[index] = jnp.zeros_like(ref[index])

    every = slice(None)
    for edge, planes2, planes1, planef in (
        (gx == 0, slice(0, 2), 0, 0),
        (gx == n_gx - 1, slice(4, 6), 3, 2),
    ):

        @pl.when(edge)
        def _(planes2=planes2, planes1=planes1, planef=planef):
            clear(coef, (every, planes2))
            clear(rhs, (every, planes1))
            clear(rbuf, (every, planes1))
            clear(fc, (every, planef))
            for k in (1, 2, 4, 5):
                clear(dirs, (k, every, planes1))

    for edge, edge_rows in ((gy == 0, slice(0, H)), (gy == n_gy - 1, slice(H + rows, ext))):

        @pl.when(edge)
        def _(edge_rows=edge_rows):
            for ref in (coef, rhs, rbuf, fc):
                clear(ref, (every, every, edge_rows))
            for k in (1, 2, 4, 5):
                clear(dirs, (k, every, every, edge_rows))

    barrier = pltpu.get_barrier_semaphore()
    expected = jnp.int32(n_gy - 1)
    for sx, sy in DIRS:
        if sx == 0:
            continue

        @pl.when(exists(sx, sy))
        def _(sx=sx, sy=sy):
            pl.semaphore_signal(
                barrier, inc=1, device_id=(gx + sx, gy + sy), device_id_type=pl.DeviceIdType.MESH
            )

        expected = expected + exists(sx, sy).astype(jnp.int32)
    for step in range(1, n_gy):
        pl.semaphore_signal(
            barrier,
            inc=1,
            device_id=(gx, lax.rem(gy + step, n_gy)),
            device_id_type=pl.DeviceIdType.MESH,
        )
    pl.semaphore_wait(barrier, expected)

    def message(ref, lead, kind, round_id, way):
        sx, sy = DIRS[way]
        if kind == "coef":
            src_p = slice(2, 4)
            dst_p = {0: slice(2, 4), 1: slice(0, 2), -1: slice(4, 6)}[sx]
        elif kind == "fine":
            src_p = {0: slice(1, 3), 1: slice(2, 3), -1: slice(1, 2)}[sx]
            dst_p = {0: slice(1, 3), 1: slice(0, 1), -1: slice(3, 4)}[sx]
        else:
            src_p = slice(1, 2)
            dst_p = {0: slice(1, 2), 1: slice(0, 1), -1: slice(2, 3)}[sx]
        src_r = {0: own, 1: slice(rows, rows + H), -1: slice(H, 2 * H)}[sy]
        dst_r = {0: own, 1: slice(0, H), -1: slice(H + rows, ext)}[sy]
        return pltpu.make_async_remote_copy(
            src_ref=ref.at[lead + (every, src_p, src_r)],
            dst_ref=ref.at[lead + (every, dst_p, dst_r)],
            send_sem=send.at[round_id, way],
            recv_sem=recv.at[round_id, way],
            device_id=(gx + sx, gy + sy),
            device_id_type=pl.DeviceIdType.MESH,
        )

    started = []

    def start(ref, lead, kind, round_id, ways):
        for way in ways:
            started.append((ref, lead, kind, round_id, way))

            @pl.when(exists(*DIRS[way]))
            def _(way=way):
                message(ref, lead, kind, round_id, way).start()

    def arrive(ref, lead, kind, round_id, ways):
        for way in ways:
            sx, sy = DIRS[way]

            @pl.when(exists(-sx, -sy))
            def _(way=way):
                message(ref, lead, kind, round_id, way).wait_recv()

    ALL = range(8)
    STAR = range(6)
    start(coef, (), "coef", 0, ALL)
    start(rhs, (), "fine", 1, ALL)

    def lane_of(count):
        return lax.broadcasted_iota(jnp.int32, (count, lanes), 1)

    def make_zshift(count, dist):
        lane = lane_of(count)

        def up(a):
            return jnp.where(lane >= lanes - dist, 0.0, pltpu.roll(a, lanes - dist, 1))

        def down(a):
            return jnp.where(lane < dist, 0.0, pltpu.roll(a, dist, 1))

        return up, down

    def coef_at(which, plane, first, count):
        return coef[which, plane, first : first + count, :]

    def operate(load, plane, first, count):
        up, down = make_zshift(count, 1)

        def mu(dp, dy):
            return coef_at(0, plane + 1 + dp, first + dy, count)

        def lam(dp, dy):
            return coef_at(1, plane + 1 + dp, first + dy, count)

        m0 = mu(0, 0)
        faces = [
            0.5 * (m0 + mu(1, 0)),
            0.5 * (m0 + mu(-1, 0)),
            0.5 * (m0 + mu(0, 1)),
            0.5 * (m0 + mu(0, -1)),
            0.5 * (m0 + up(m0)),
            0.5 * (m0 + down(m0)),
        ]
        centre = [load(c, plane, 0, 0) for c in range(3)]
        vx_up = load(0, plane, 1, 0)
        vy_up = load(1, plane, 0, 1)
        vz_up = up(centre[2])
        here = lam(0, 0) * (
            (vx_up - centre[0]) + (vy_up - centre[1]) + (vz_up - centre[2])
        )
        vx_low = load(0, plane, -1, 0)
        vy_side = load(1, plane, -1, 0)
        vz_side = load(2, plane, -1, 0)
        back_x = lam(-1, 0) * (
            (centre[0] - vx_low)
            + (load(1, plane, -1, 1) - vy_side)
            + (up(vz_side) - vz_side)
        )
        vx_below = load(0, plane, 0, -1)
        vy_low = load(1, plane, 0, -1)
        vz_below = load(2, plane, 0, -1)
        back_y = lam(0, -1) * (
            (load(0, plane, 1, -1) - vx_below)
            + (centre[1] - vy_low)
            + (up(vz_below) - vz_below)
        )
        backs = [back_x, back_y, down(here)]
        out = []
        for c in range(3):
            v = centre[c]
            laplace = (
                faces[0] * ((vx_up if c == 0 else load(c, plane, 1, 0)) - v)
                - faces[1] * (v - load(c, plane, -1, 0))
                + faces[2] * ((vy_up if c == 1 else load(c, plane, 0, 1)) - v)
                - faces[3] * (v - load(c, plane, 0, -1))
                + faces[4] * ((vz_up if c == 2 else up(v)) - v)
                - faces[5] * (v - down(v))
            )
            out.append(-laplace - (here - backs[c]))
        return out

    def direction_load(k, first, count):
        def load(c, plane, dp, dy):
            return dirs[k, c, plane + dp, first + dy : first + dy + count, :]

        return load

    steps = weights(SWEEPS)

    arrive(coef, (), "coef", 0, ALL)
    wide_first, wide = H - 1, rows + 2
    up, down = make_zshift(wide, 1)
    row_id = lax.broadcasted_iota(jnp.int32, (wide, lanes), 0)
    row_ok = jnp.logical_and(
        jnp.logical_or(row_id > 0, gy > 0), jnp.logical_or(row_id < wide - 1, gy < n_gy - 1)
    )
    for plane in range(4):
        m0 = coef_at(0, plane + 1, wide_first, wide)
        l0 = coef_at(1, plane + 1, wide_first, wide)
        total = (
            0.5 * (m0 + coef_at(0, plane + 2, wide_first, wide))
            + 0.5 * (m0 + coef_at(0, plane, wide_first, wide))
            + 0.5 * (m0 + coef_at(0, plane + 1, wide_first + 1, wide))
            + 0.5 * (m0 + coef_at(0, plane + 1, wide_first - 1, wide))
            + 0.5 * (m0 + up(m0))
            + 0.5 * (m0 + down(m0))
            + l0
        )
        sides = (
            coef_at(1, plane, wide_first, wide),
            coef_at(1, plane + 1, wide_first - 1, wide),
            down(l0),
        )
        ok = row_ok
        if plane == 0:
            ok = jnp.logical_and(ok, gx > 0)
        if plane == 3:
            ok = jnp.logical_and(ok, gx < n_gx - 1)
        for c in range(3):
            inv[c, plane, wide_first : wide_first + wide, :] = jnp.where(
                ok, 1.0 / (total + sides[c]), 0.0
            )
    arrive(rhs, (), "fine", 1, ALL)
    wide_rows = slice(wide_first, wide_first + wide)
    for plane in range(4):
        for c in range(3):
            dirs[0, c, plane, wide_rows, :] = (
                steps[0][1] * inv[c, plane, wide_rows, :] * rhs[c, plane, wide_rows, :]
            )

    def relax(k, source, target, following):
        for plane in (1, 2):
            applied = operate(direction_load(k, H, rows), plane, H, rows)
            for c in range(3):
                left = source(c, plane) - applied[c]
                target(c, plane, left)
                if following is not None:
                    dirs[k + 1, c, plane, own, :] = (
                        following[0] * dirs[k, c, plane, own, :]
                        + following[1] * (inv[c, plane, own, :] * left)
                    )

    def into_rbuf(c, plane, value):
        rbuf[c, plane, own, :] = value

    def from_rbuf(c, plane):
        return rbuf[c, plane, own, :]

    relax(0, lambda c, plane: rhs[c, plane, own, :], into_rbuf, steps[1])
    start(dirs, (1,), "fine", 2, STAR)

    lane = lane_of(ext)
    rid = lax.broadcasted_iota(jnp.int32, (ext, lanes), 0)
    lane_even = lane % 2 == 0
    row_even = rid % 2 == 0

    def cube_sum(a):
        a = a + jnp.where(lane_even, pltpu.roll(a, lanes - 1, 1), pltpu.roll(a, 1, 1))
        return a + jnp.where(row_even, pltpu.roll(a, ext - 1, 0), pltpu.roll(a, 1, 0))

    labels = []
    label = jnp.int32(0)
    for j in range(n_gy):
        if j > 0:
            label = label + starts_ref[0, j]
        labels.append(label)
    mine = labels[0]
    before = labels[0] - 1
    after = labels[0] - 1
    for j in range(n_gy):
        mine = jnp.where(gy == j, labels[j], mine)
        if j > 0:
            before = jnp.where(gy == j, labels[j - 1], before)
        if j < n_gy - 1:
            after = jnp.where(gy == j, labels[j + 1], after)
    low_open = jnp.logical_and(gy > 0, before == mine)
    high_open = jnp.logical_and(gy < n_gy - 1, after == mine)
    inside = jnp.logical_and(
        jnp.logical_or(rid >= H, low_open), jnp.logical_or(rid < H + rows, high_open)
    )
    up2, down2 = make_zshift(ext, 2)

    def row_up(a):
        return pltpu.roll(a, ext - 2, 0)

    def row_down(a):
        return pltpu.roll(a, 2, 0)

    cmu = jnp.where(inside, 0.125 * cube_sum(coef[0, 2] + coef[0, 3]), 0.0)
    clam = jnp.where(inside, 0.125 * cube_sum(coef[1, 2] + coef[1, 3]), 0.0)
    cf = [
        0.5 * (cmu + row_up(cmu)),
        0.5 * (cmu + row_down(cmu)),
        0.5 * (cmu + up2(cmu)),
        0.5 * (cmu + down2(cmu)),
    ]
    csum = cmu + cf[0] + cf[1] + cf[2] + cf[3]
    cinv = [
        jnp.where(inside, 1.0 / (4.0 * (csum + clam + side)), 0.0)
        for side in (0.0, row_down(clam), down2(clam))
    ]

    def coarse_operate(v):
        vy_up = row_up(v[1])
        vz_up = up2(v[2])
        here = clam * ((vy_up - v[1]) + (vz_up - v[2]) - v[0])
        backs = [0.0, row_down(here), down2(here)]
        out = []
        for c in range(3):
            laplace = (
                cf[0] * ((vy_up if c == 1 else row_up(v[c])) - v[c])
                - cf[1] * (v[c] - row_down(v[c]))
                + cf[2] * ((vz_up if c == 2 else up2(v[c])) - v[c])
                - cf[3] * (v[c] - down2(v[c]))
                - cmu * v[c]
            )
            out.append(4.0 * (-laplace - (here - backs[c])))
        return out

    for c in range(3):
        for plane in (1, 2):
            sol_ref[c, plane - 1] = dirs[0, c, plane, own, :] + dirs[1, c, plane, own, :]
    arrive(dirs, (1,), "fine", 2, STAR)
    relax(1, from_rbuf, into_rbuf, steps[2])
    start(dirs, (2,), "fine", 3, STAR)
    for c in range(3):
        for plane in (1, 2):
            sol_ref[c, plane - 1] += dirs[2, c, plane, own, :]
    arrive(dirs, (2,), "fine", 3, STAR)
    relax(2, from_rbuf, into_rbuf, None)
    start(rbuf, (), "fine", 4, (2, 3, 0, 1, 4, 5, 6, 7))

    sub = lax.broadcasted_iota(jnp.int32, (8, lanes), 0)
    part = jnp.zeros((8, lanes), jnp.float32)
    for c in range(3):
        both = rbuf[c, 1, own, :] + rbuf[c, 2, own, :]
        part = jnp.where(sub == c, jnp.sum(both, axis=0, keepdims=True), part)
    sums[0] = part

    def sum_message(step):
        return pltpu.make_async_remote_copy(
            src_ref=sums.at[0],
            dst_ref=sums.at[step],
            send_sem=sum_send.at[step],
            recv_sem=sum_recv.at[step],
            device_id=(gx, lax.rem(gy + step, n_gy)),
            device_id_type=pl.DeviceIdType.MESH,
        )

    for step in range(1, n_gy):
        sum_message(step).start()

    arrive(rbuf, (), "fine", 4, (2, 3))
    left = [
        jnp.where(inside, cube_sum(rbuf[c, 1] + rbuf[c, 2]), 0.0) for c in range(3)
    ]
    coarse_steps = weights(COARSE_SWEEPS)
    direction = [coarse_steps[0][1] * cinv[c] * left[c] for c in range(3)]
    smoothed = direction
    for old, new in coarse_steps[1:]:
        applied = coarse_operate(direction)
        left = [left[c] - applied[c] for c in range(3)]
        direction = [old * direction[c] + new * (cinv[c] * left[c]) for c in range(3)]
        smoothed = [smoothed[c] + direction[c] for c in range(3)]

    total = sums[0]
    members = jnp.float32(1.0)
    for step in range(1, n_gy):
        sum_message(step).wait_recv()
        source = lax.rem(gy + n_gy - step, n_gy)
        other = labels[0]
        for j in range(1, n_gy):
            other = jnp.where(source == j, labels[j], other)
        same = jnp.where(other == mine, jnp.float32(1.0), jnp.float32(0.0))
        total = total + same * sums[step]
        members = members + same
    cells_dev = (rows // 2) * (lanes // 2)
    scale = jnp.full((8, 1), SHIFT_SCALE * cells_dev, jnp.float32) * members
    shift = jnp.sum(total, axis=1, keepdims=True) / scale
    for c in range(3):
        fc[c, 1, own, :] = smoothed[c][H : H + rows] + shift[c : c + 1, :]
    start(fc, (), "coarse", 5, ALL)
    for c in range(3):
        for plane in (1, 2):
            sol_ref[c, plane - 1] += fc[c, 1, own, :]
    arrive(rbuf, (), "fine", 4, (0, 1, 4, 5, 6, 7))
    arrive(fc, (), "coarse", 5, ALL)

    def fc_load(c, plane, dp, dy):
        return fc[c, (plane + 1 + dp) // 2, wide_first + dy : wide_first + dy + wide, :]

    for plane in range(4):
        applied = operate(fc_load, plane, wide_first, wide)
        for c in range(3):
            value = rbuf[c, plane, wide_rows, :] - applied[c]
            r2buf[c, plane, wide_rows, :] = value
            dirs[3, c, plane, wide_rows, :] = steps[0][1] * inv[c, plane, wide_rows, :] * value

    def into_r2(c, plane, value):
        r2buf[c, plane, own, :] = value

    def from_r2(c, plane):
        return r2buf[c, plane, own, :]

    def into_result(c, plane, value):
        res_ref[c, plane - 1] = value

    relax(3, from_r2, into_r2, steps[1])
    start(dirs, (4,), "fine", 6, STAR)
    for c in range(3):
        for plane in (1, 2):
            sol_ref[c, plane - 1] += dirs[3, c, plane, own, :] + dirs[4, c, plane, own, :]
    arrive(dirs, (4,), "fine", 6, STAR)
    relax(4, from_r2, into_r2, steps[2])
    start(dirs, (5,), "fine", 7, STAR)
    for c in range(3):
        for plane in (1, 2):
            sol_ref[c, plane - 1] += dirs[5, c, plane, own, :]
    arrive(dirs, (5,), "fine", 7, STAR)
    relax(5, from_r2, into_result, None)

    for ref, lead, kind, round_id, way in started:

        @pl.when(exists(*DIRS[way]))
        def _(ref=ref, lead=lead, kind=kind, round_id=round_id, way=way):
            message(ref, lead, kind, round_id, way).wait_send()

    for step in range(1, n_gy):
        sum_message(step).wait_send()


def solution(mesh):
    n_gx = mesh.shape["gx"]
    n_gy = mesh.shape["gy"]

    def shards(rhs_field, shear_modulus, lame_lambda, group_start):
        _, planes, rows, lanes = rhs_field.shape
        assert planes == 2
        ext = rows + 2 * H
        vmem = pl.BlockSpec(memory_space=pltpu.VMEM)
        field = jax.ShapeDtypeStruct(rhs_field.shape, jnp.float32)
        f32 = jnp.float32
        return pl.pallas_call(
            functools.partial(kernel, n_gx, n_gy),
            out_shape=(field, field),
            in_specs=[vmem, vmem, vmem, pl.BlockSpec(memory_space=pltpu.SMEM)],
            out_specs=(vmem, vmem),
            scratch_shapes=[
                pltpu.VMEM((2, 6, ext, lanes), f32),
                pltpu.VMEM((3, 4, ext, lanes), f32),
                pltpu.VMEM((3, 4, ext, lanes), f32),
                pltpu.VMEM((6, 3, 4, ext, lanes), f32),
                pltpu.VMEM((3, 4, ext, lanes), f32),
                pltpu.VMEM((3, 4, ext, lanes), f32),
                pltpu.VMEM((3, 3, ext, lanes), f32),
                pltpu.VMEM((n_gy, 8, lanes), f32),
                pltpu.SemaphoreType.DMA((8, 8)),
                pltpu.SemaphoreType.DMA((8, 8)),
                pltpu.SemaphoreType.DMA((n_gy,)),
                pltpu.SemaphoreType.DMA((n_gy,)),
            ],
            compiler_params=pltpu.CompilerParams(
                collective_id=0, has_side_effects=True, vmem_limit_bytes=24 * 1024 * 1024
            ),
            cost_estimate=pl.CostEstimate(
                flops=10_000_000, bytes_accessed=400_000, transcendentals=0
            ),
        )(rhs_field, shear_modulus, lame_lambda, group_start)

    return jax.shard_map(
        shards,
        mesh=mesh,
        in_specs=(
            P(None, "gx", "gy", None),
            P("gx", "gy", None),
            P("gx", "gy", None),
            P("gx", None),
        ),
        out_specs=(P(None, "gx", "gy", None), P(None, "gx", "gy", None)),
        check_vma=False,
    )
```

time: 178 us -> 39.1 us (0.22)
  starting transfers between devices: 76.9 us -> 0 us
  waiting for transfers between devices: 49 us -> 0 us
  Pallas kernels: 0 us -> 33.8 us
  other arithmetic: 22.8 us -> 0 us
  blocking collectives: 11.4 us -> 0 us
  local copies, waits for them, and re-layouts: 13.9 us -> 4.34 us
  between operations: 2.56 us -> 0.65 us
    ppermute x32 -> x0, starting transfers between devices: 76.9 us -> none  [the longest x16 50.6 us: padded_2(): lax.ppermute(lax.slice_in_dim(block, block.shape[dim] - width, None, axis...]
    ppermute x32 -> x0, waiting for transfers between devices: 49 us -> none  [the longest x16 48.9 us: padded_2(): lax.ppermute(lax.slice_in_dim(block, 0, width, axis=dim), axis, backward)]
    pallas_call x0 -> x1, Pallas kernels: none -> 33.8 us  [shards(): pl.pallas_call(functools.partial(kernel, n_gx, n_gy), out_shape=(field, f...]
    all_gather x1 -> x0, blocking collectives: 11.4 us -> none  [shards(): column = lax.all_gather(packed, 'gy', axis=1, tiled=True)]
    another operation x36 -> x0, other arithmetic: 6.41 us -> none  [the longest x30 4.99 us: operate(): return jnp.stack(results)]
    reduce_sum x3 -> x0, local copies, waits for them, and re-layouts: 5.89 us -> none  [the longest x1 3.89 us: shards(): residual.reshape(3, coarse_x, 2, coarse_y, 2, coarse_z, 2)]
    concatenate x14 -> x0, other arithmetic: 5.41 us -> none  [the longest x8 3.52 us: padded_2(): block = jnp.concatenate([low, block, high], axis=dim)]
    reduce_sum x9 -> x0, other arithmetic: 4.29 us -> none  [the longest x2 1.71 us: shards(): residual.reshape(3, coarse_x, 2, coarse_y, 2, coarse_z, 2)]
  transfers between devices with their start and end apart: 32 -> 0, of which waited for: 15 -> 0; matrix products, arithmetic and copies ran while one was open for 5% -> 0% of each run, Pallas kernels for 0% -> 0%
where the time goes in v1:
time: 39.1 us; the launch traced here: 38.8 us
  Pallas kernels  33.8 us (86%)
  local copies, waits for them, and re-layouts  4.34 us (11%)
  between operations  0.65 us (2%)
    pallas_call x1, Pallas kernels, shards(): pl.pallas_call(functools.partial(kernel, n_gx, n_gy), out_shape=(field, f...  33.8 us
    unnamed x10, local copies, waits for them, and re-layouts  4.34 us

profile of v1, /device:TPU:3, one launch (start us, length us, event | category | flops | bytes accessed | tf_op | source)
XLA Modules:
  0.0 38.8 jit_solution(11242636113391805678)
XLA Ops:
  0.6 0.0 copy-start
  0.6 0.9 %copy-done = f32[3,2,32,128]{3,2,1,0:T(8,128)S(1)} copy-done((f32[3,2,32,128]{3,2,1,0:T(8,128)S(1)}, f32[3,2,32,128]{3,2,1,0:T(8,128)}, u32[]{:S(2)}) %copy-start) | copy-done | bytes 98328
  1.5 0.0 copy-start.1
  1.5 0.8 %copy-done.1 = f32[2,32,128]{2,1,0:T(8,128)S(1)} copy-done((f32[2,32,128]{2,1,0:T(8,128)S(1)}, f32[2,32,128]{2,1,0:T(8,128)}, u32[]{:S(2)}) %copy-start.1) | copy-done | bytes 32792
  2.3 0.0 copy-start.2
  2.3 0.8 %copy-done.2 = f32[2,32,128]{2,1,0:T(8,128)S(1)} copy-done((f32[2,32,128]{2,1,0:T(8,128)S(1)}, f32[2,32,128]{2,1,0:T(8,128)}, u32[]{:S(2)}) %copy-start.2) | copy-done | bytes 32792
  3.0 0.0 copy-start.3
  3.0 0.7 %copy-done.3 = s32[1,4]{1,0:T(1,128)S(1)} copy-done((s32[1,4]{1,0:T(1,128)S(1)}, s32[1,4]{1,0:T(1,128)}, u32[]{:S(2)}) %copy-start.3) | copy-done | bytes 40
  3.7 33.8 %shard_map.59 = (f32[3,2,32,128]{3,2,1,0:T(8,128)S(1)}, f32[3,2,32,128]{3,2,1,0:T(8,128)S(1)}) custom-call(f32[3,2,32,128]{3,2,1,0:T(8,128)S(1)} %copy-done, f32[2,32,128]{2,1,0:T(8,128)S(1)} %copy-done.1, f32[2,32,128]{2,1,0:T(8,128)S(1)} %copy-done.2, s32[1,4]{1,0:T(1,128)S(1)} %copy-done.3), custom_call_target="tpu_custom_call" | custom-call | flops 10000000 | bytes 400000 | tf_op jit(solution)/shard_map/pallas_call | solution.py:489
  37.5 0.6 %copy.8 = f32[3,2,32,128]{3,2,1,0:T(8,128)} copy(f32[3,2,32,128]{3,2,1,0:T(8,128)S(1)} %get-tuple-element.4) | data formatting | bytes 196608
  38.2 0.6 %copy.9 = f32[3,2,32,128]{3,2,1,0:T(8,128)} copy(f32[3,2,32,128]{3,2,1,0:T(8,128)S(1)} %get-tuple-element.5) | data formatting | bytes 196608
Async XLA Ops:
  0.6 0.9 %copy-start = (f32[3,2,32,128]{3,2,1,0:T(8,128)S(1)}, f32[3,2,32,128]{3,2,1,0:T(8,128)}, u32[]{:S(2)}) copy-start(f32[3,2,32,128]{3,2,1,0:T(8,128)} %rhs_ref.1) | copy-start | bytes 294916
  1.5 0.8 %copy-start.1 = (f32[2,32,128]{2,1,0:T(8,128)S(1)}, f32[2,32,128]{2,1,0:T(8,128)}, u32[]{:S(2)}) copy-start(f32[2,32,128]{2,1,0:T(8,128)} %mu_ref.1) | copy-start | bytes 98308
  2.3 0.8 %copy-start.2 = (f32[2,32,128]{2,1,0:T(8,128)S(1)}, f32[2,32,128]{2,1,0:T(8,128)}, u32[]{:S(2)}) copy-start(f32[2,32,128]{2,1,0:T(8,128)} %lam_ref.1) | copy-start | bytes 98308
  3.0 0.7 %copy-start.3 = (s32[1,4]{1,0:T(1,128)S(1)}, s32[1,4]{1,0:T(1,128)}, u32[]{:S(2)}) copy-start(s32[1,4]{1,0:T(1,128)} %starts_ref.1) | copy-start | bytes 52

commit v2 on v1

--- a/solution.py
+++ b/solution.py
@@ -32,11 +32,11 @@
 
 
 def kernel(
-    n_gx, n_gy, rhs_ref, mu_ref, lam_ref, starts_ref, sol_ref, res_ref,
-    coef, rhs, inv, dirs, rbuf, r2buf, fc, sums, send, recv, sum_send, sum_recv,
+    n_gx, n_gy, rhs_in, mu_in, lam_in, starts_in, sol_ref, res_ref,
+    coef, rhs, inv, dirs, rbuf, r2buf, fc, sums, starts_ref, send, recv, sum_send, sum_recv, load_sem,
 ):
-    rows = rhs_ref.shape[2]
-    lanes = rhs_ref.shape[3]
+    rows = rhs_in.shape[2]
+    lanes = rhs_in.shape[3]
     ext = rows + 2 * H
     gx = lax.axis_index("gx")
     gy = lax.axis_index("gy")
@@ -54,9 +54,39 @@
             ok = here if ok is None else jnp.logical_and(ok, here)
         return ok
 
-    coef[0, 2:4, own, :] = mu_ref[...]
-    coef[1, 2:4, own, :] = lam_ref[...]
-    rhs[:, 1:3, own, :] = rhs_ref[...]
+    barrier = pltpu.get_barrier_semaphore()
+    expected = jnp.int32(n_gy - 1)
+    for sx, sy in DIRS:
+        if sx == 0:
+            continue
+
+        @pl.when(exists(sx, sy))
+        def _(sx=sx, sy=sy):
+            pl.semaphore_signal(
+                barrier, inc=1, device_id=(gx + sx, gy + sy), device_id_type=pl.DeviceIdType.MESH
+            )
+
+        expected = expected + exists(sx, sy).astype(jnp.int32)
+    for step in range(1, n_gy):
+        pl.semaphore_signal(
+            barrier,
+            inc=1,
+            device_id=(gx, lax.rem(gy + step, n_gy)),
+            device_id_type=pl.DeviceIdType.MESH,
+        )
+    loads = [
+        pltpu.make_async_copy(source, target, load_sem.at[k])
+        for k, (source, target) in enumerate(
+            (
+                (mu_in, coef.at[0, 2:4, own]),
+                (lam_in, coef.at[1, 2:4, own]),
+                (rhs_in, rhs.at[:, 1:3, own]),
+                (starts_in, starts_ref),
+            )
+        )
+    ]
+    for copy in loads:
+        copy.start()
 
     def clear(ref, index):
         ref[index] = jnp.zeros_like(ref[index])
@@ -85,26 +115,8 @@
             for k in (1, 2, 4, 5):
                 clear(dirs, (k, every, every, edge_rows))
 
-    barrier = pltpu.get_barrier_semaphore()
-    expected = jnp.int32(n_gy - 1)
-    for sx, sy in DIRS:
-        if sx == 0:
-            continue
-
-        @pl.when(exists(sx, sy))
-        def _(sx=sx, sy=sy):
-            pl.semaphore_signal(
-                barrier, inc=1, device_id=(gx + sx, gy + sy), device_id_type=pl.DeviceIdType.MESH
-            )
-
-        expected = expected + exists(sx, sy).astype(jnp.int32)
-    for step in range(1, n_gy):
-        pl.semaphore_signal(
-            barrier,
-            inc=1,
-            device_id=(gx, lax.rem(gy + step, n_gy)),
-            device_id_type=pl.DeviceIdType.MESH,
-        )
+    for copy in loads:
+        copy.wait()
     pl.semaphore_wait(barrier, expected)
 
     def message(ref, lead, kind, round_id, way):
@@ -484,12 +496,13 @@
         assert planes == 2
         ext = rows + 2 * H
         vmem = pl.BlockSpec(memory_space=pltpu.VMEM)
+        hbm = pl.BlockSpec(memory_space=pltpu.MemorySpace.HBM)
         field = jax.ShapeDtypeStruct(rhs_field.shape, jnp.float32)
         f32 = jnp.float32
         return pl.pallas_call(
             functools.partial(kernel, n_gx, n_gy),
             out_shape=(field, field),
-            in_specs=[vmem, vmem, vmem, pl.BlockSpec(memory_space=pltpu.SMEM)],
+            in_specs=[hbm, hbm, hbm, hbm],
             out_specs=(vmem, vmem),
             scratch_shapes=[
                 pltpu.VMEM((2, 6, ext, lanes), f32),
@@ -500,10 +513,12 @@
                 pltpu.VMEM((3, 4, ext, lanes), f32),
                 pltpu.VMEM((3, 3, ext, lanes), f32),
                 pltpu.VMEM((n_gy, 8, lanes), f32),
+                pltpu.SMEM((1, n_gy), jnp.int32),
                 pltpu.SemaphoreType.DMA((8, 8)),
                 pltpu.SemaphoreType.DMA((8, 8)),
                 pltpu.SemaphoreType.DMA((n_gy,)),
                 pltpu.SemaphoreType.DMA((n_gy,)),
+                pltpu.SemaphoreType.DMA((4,)),
             ],
             compiler_params=pltpu.CompilerParams(
                 collective_id=0, has_side_effects=True, vmem_limit_bytes=24 * 1024 * 1024

time: 39.1 us -> 38.5 us (0.985)
  Pallas kernels: 33.8 us -> 33.2 us
    pallas_call x1, Pallas kernels: 33.8 us -> 33.2 us  [shards(): pl.pallas_call(functools.partial(kernel, n_gx, n_gy), out_shape=(field, f...]
where the time goes in v2:
time: 38.5 us; the launch traced here: 38.2 us
  Pallas kernels  33.2 us (86%)
  local copies, waits for them, and re-layouts  4.34 us (11%)
  between operations  0.65 us (2%)
    pallas_call x1, Pallas kernels, shards(): pl.pallas_call(functools.partial(kernel, n_gx, n_gy), out_shape=(field, f...  33.2 us
    unnamed x10, local copies, waits for them, and re-layouts  4.34 us

profile of v2, /device:TPU:3, one launch (start us, length us, event | category | flops | bytes accessed | tf_op | source)
XLA Modules:
  0.0 38.2 jit_solution(7175169080414129846)
XLA Ops:
  0.6 0.0 copy-start
  0.6 0.9 %copy-done = f32[3,2,32,128]{3,2,1,0:T(8,128)S(1)} copy-done((f32[3,2,32,128]{3,2,1,0:T(8,128)S(1)}, f32[3,2,32,128]{3,2,1,0:T(8,128)}, u32[]{:S(2)}) %copy-start) | copy-done | bytes 98328
  1.5 0.0 copy-start.1
  1.5 0.8 %copy-done.1 = f32[2,32,128]{2,1,0:T(8,128)S(1)} copy-done((f32[2,32,128]{2,1,0:T(8,128)S(1)}, f32[2,32,128]{2,1,0:T(8,128)}, u32[]{:S(2)}) %copy-start.1) | copy-done | bytes 32792
  2.3 0.0 copy-start.2
  2.3 0.8 %copy-done.2 = f32[2,32,128]{2,1,0:T(8,128)S(1)} copy-done((f32[2,32,128]{2,1,0:T(8,128)S(1)}, f32[2,32,128]{2,1,0:T(8,128)}, u32[]{:S(2)}) %copy-start.2) | copy-done | bytes 32792
  3.0 0.0 copy-start.3
  3.0 0.7 %copy-done.3 = s32[1,4]{1,0:T(1,128)S(1)} copy-done((s32[1,4]{1,0:T(1,128)S(1)}, s32[1,4]{1,0:T(1,128)}, u32[]{:S(2)}) %copy-start.3) | copy-done | bytes 40
  3.7 33.2 %shard_map.59 = (f32[3,2,32,128]{3,2,1,0:T(8,128)S(1)}, f32[3,2,32,128]{3,2,1,0:T(8,128)S(1)}) custom-call(f32[3,2,32,128]{3,2,1,0:T(8,128)S(1)} %copy-done, f32[2,32,128]{2,1,0:T(8,128)S(1)} %copy-done.1, f32[2,32,128]{2,1,0:T(8,128)S(1)} %copy-done.2, s32[1,4]{1,0:T(1,128)S(1)} %copy-done.3), custom_call_target="tpu_custom_call" | custom-call | flops 10000000 | bytes 400000 | tf_op jit(solution)/shard_map/pallas_call | solution.py:502
  36.9 0.6 %copy.8 = f32[3,2,32,128]{3,2,1,0:T(8,128)} copy(f32[3,2,32,128]{3,2,1,0:T(8,128)S(1)} %get-tuple-element.4) | data formatting | bytes 196608
  37.6 0.6 %copy.9 = f32[3,2,32,128]{3,2,1,0:T(8,128)} copy(f32[3,2,32,128]{3,2,1,0:T(8,128)S(1)} %get-tuple-element.5) | data formatting | bytes 196608
Async XLA Ops:
  0.6 0.9 %copy-start = (f32[3,2,32,128]{3,2,1,0:T(8,128)S(1)}, f32[3,2,32,128]{3,2,1,0:T(8,128)}, u32[]{:S(2)}) copy-start(f32[3,2,32,128]{3,2,1,0:T(8,128)} %rhs_in.1) | copy-start | bytes 294916
  1.5 0.8 %copy-start.1 = (f32[2,32,128]{2,1,0:T(8,128)S(1)}, f32[2,32,128]{2,1,0:T(8,128)}, u32[]{:S(2)}) copy-start(f32[2,32,128]{2,1,0:T(8,128)} %mu_in.1) | copy-start | bytes 98308
  2.3 0.8 %copy-start.2 = (f32[2,32,128]{2,1,0:T(8,128)S(1)}, f32[2,32,128]{2,1,0:T(8,128)}, u32[]{:S(2)}) copy-start(f32[2,32,128]{2,1,0:T(8,128)} %lam_in.1) | copy-start | bytes 98308
  3.0 0.7 %copy-start.3 = (s32[1,4]{1,0:T(1,128)S(1)}, s32[1,4]{1,0:T(1,128)}, u32[]{:S(2)}) copy-start(s32[1,4]{1,0:T(1,128)} %starts_in.1) | copy-start | bytes 52

commit v3 on v2

--- a/solution.py
+++ b/solution.py
@@ -18,7 +18,8 @@
 SIGMA = MID / HALF
 
 H = 8
-DIRS = ((1, 0), (-1, 0), (0, 1), (0, -1), (1, -1), (-1, 1), (1, 1), (-1, -1))
+DIRS = ((1, 0), (-1, 0), (0, 1), (0, -1), (1, -1), (-1, 1), (1, 1), (-1, -1),
+        (2, 0), (-2, 0), (2, -1), (-2, 1))
 
 
 def weights(steps):
@@ -45,12 +46,9 @@
     def exists(sx, sy):
         ok = None
         for pos, step, count in ((gx, sx, n_gx), (gy, sy, n_gy)):
-            if step == 1:
-                here = pos < count - 1
-            elif step == -1:
-                here = pos > 0
-            else:
+            if step == 0:
                 continue
+            here = pos < count - step if step > 0 else pos >= -step
             ok = here if ok is None else jnp.logical_and(ok, here)
         return ok
 
@@ -78,9 +76,9 @@
         pltpu.make_async_copy(source, target, load_sem.at[k])
         for k, (source, target) in enumerate(
             (
-                (mu_in, coef.at[0, 2:4, own]),
-                (lam_in, coef.at[1, 2:4, own]),
-                (rhs_in, rhs.at[:, 1:3, own]),
+                (mu_in, coef.at[0, 3:5, own]),
+                (lam_in, coef.at[1, 3:5, own]),
+                (rhs_in, rhs.at[:, 2:4, own]),
                 (starts_in, starts_ref),
             )
         )
@@ -93,8 +91,8 @@
 
     every = slice(None)
     for edge, planes2, planes1, planef in (
-        (gx == 0, slice(0, 2), 0, 0),
-        (gx == n_gx - 1, slice(4, 6), 3, 2),
+        (gx == 0, slice(0, 3), slice(0, 2), slice(0, 2)),
+        (gx == n_gx - 1, slice(5, 8), slice(4, 6), slice(3, 5)),
     ):
 
         @pl.when(edge)
@@ -103,8 +101,15 @@
             clear(rhs, (every, planes1))
             clear(rbuf, (every, planes1))
             clear(fc, (every, planef))
-            for k in (1, 2, 4, 5):
+            for k in (2, 5):
                 clear(dirs, (k, every, planes1))
+
+    for edge, plane_c, plane_f in ((gx == 1, 0, 0), (gx == n_gx - 2, 7, 4)):
+
+        @pl.when(edge)
+        def _(plane_c=plane_c, plane_f=plane_f):
+            clear(coef, (every, plane_c))
+            clear(fc, (every, plane_f))
 
     for edge, edge_rows in ((gy == 0, slice(0, H)), (gy == n_gy - 1, slice(H + rows, ext))):
 
@@ -112,7 +117,7 @@
         def _(edge_rows=edge_rows):
             for ref in (coef, rhs, rbuf, fc):
                 clear(ref, (every, every, edge_rows))
-            for k in (1, 2, 4, 5):
+            for k in (2, 5):
                 clear(dirs, (k, every, every, edge_rows))
 
     for copy in loads:
@@ -122,14 +127,21 @@
     def message(ref, lead, kind, round_id, way):
         sx, sy = DIRS[way]
         if kind == "coef":
+            src_p = {2: slice(4, 5), -2: slice(3, 4)}.get(sx, slice(3, 5))
+            dst_p = {
+                0: slice(3, 5), 1: slice(1, 3), -1: slice(5, 7), 2: slice(0, 1), -2: slice(7, 8)
+            }[sx]
+        elif kind == "deep":
             src_p = slice(2, 4)
             dst_p = {0: slice(2, 4), 1: slice(0, 2), -1: slice(4, 6)}[sx]
         elif kind == "fine":
-            src_p = {0: slice(1, 3), 1: slice(2, 3), -1: slice(1, 2)}[sx]
-            dst_p = {0: slice(1, 3), 1: slice(0, 1), -1: slice(3, 4)}[sx]
+            src_p = {0: slice(2, 4), 1: slice(3, 4), -1: slice(2, 3)}[sx]
+            dst_p = {0: slice(2, 4), 1: slice(1, 2), -1: slice(4, 5)}[sx]
         else:
-            src_p = slice(1, 2)
-            dst_p = {0: slice(1, 2), 1: slice(0, 1), -1: slice(2, 3)}[sx]
+            src_p = slice(2, 3)
+            dst_p = {
+                0: slice(2, 3), 1: slice(1, 2), -1: slice(3, 4), 2: slice(0, 1), -2: slice(4, 5)
+            }[sx]
         src_r = {0: own, 1: slice(rows, rows + H), -1: slice(H, 2 * H)}[sy]
         dst_r = {0: own, 1: slice(0, H), -1: slice(H + rows, ext)}[sy]
         return pltpu.make_async_remote_copy(
@@ -159,10 +171,11 @@
             def _(way=way):
                 message(ref, lead, kind, round_id, way).wait_recv()
 
-    ALL = range(8)
+    ALL = range(12)
+    NEAR = range(8)
     STAR = range(6)
     start(coef, (), "coef", 0, ALL)
-    start(rhs, (), "fine", 1, ALL)
+    start(rhs, (), "deep", 1, NEAR)
 
     def lane_of(count):
         return lax.broadcasted_iota(jnp.int32, (count, lanes), 1)
@@ -246,13 +259,13 @@
     steps = weights(SWEEPS)
 
     arrive(coef, (), "coef", 0, ALL)
-    wide_first, wide = H - 1, rows + 2
+    wide_first, wide = H - 2, rows + 4
     up, down = make_zshift(wide, 1)
     row_id = lax.broadcasted_iota(jnp.int32, (wide, lanes), 0)
     row_ok = jnp.logical_and(
-        jnp.logical_or(row_id > 0, gy > 0), jnp.logical_or(row_id < wide - 1, gy < n_gy - 1)
+        jnp.logical_or(row_id > 1, gy > 0), jnp.logical_or(row_id < wide - 2, gy < n_gy - 1)
     )
-    for plane in range(4):
+    for plane in range(6):
         m0 = coef_at(0, plane + 1, wide_first, wide)
         l0 = coef_at(1, plane + 1, wide_first, wide)
         total = (
@@ -270,42 +283,43 @@
             down(l0),
         )
         ok = row_ok
-        if plane == 0:
+        if plane < 2:
             ok = jnp.logical_and(ok, gx > 0)
-        if plane == 3:
+        if plane > 3:
             ok = jnp.logical_and(ok, gx < n_gx - 1)
         for c in range(3):
             inv[c, plane, wide_first : wide_first + wide, :] = jnp.where(
                 ok, 1.0 / (total + sides[c]), 0.0
             )
-    arrive(rhs, (), "fine", 1, ALL)
+    arrive(rhs, (), "deep", 1, NEAR)
     wide_rows = slice(wide_first, wide_first + wide)
-    for plane in range(4):
+    for plane in range(6):
         for c in range(3):
             dirs[0, c, plane, wide_rows, :] = (
                 steps[0][1] * inv[c, plane, wide_rows, :] * rhs[c, plane, wide_rows, :]
             )
 
-    def relax(k, source, target, following):
-        for plane in (1, 2):
-            applied = operate(direction_load(k, H, rows), plane, H, rows)
+    def relax(k, source, target, following, planes, first, count):
+        some = slice(first, first + count)
+        for plane in planes:
+            applied = operate(direction_load(k, first, count), plane, first, count)
             for c in range(3):
-                left = source(c, plane) - applied[c]
-                target(c, plane, left)
+                left = source[c, plane, some, :] - applied[c]
+                if target is None:
+                    res_ref[c, plane - 2] = left
+                else:
+                    target[c, plane, some, :] = left
                 if following is not None:
-                    dirs[k + 1, c, plane, own, :] = (
-                        following[0] * dirs[k, c, plane, own, :]
-                        + following[1] * (inv[c, plane, own, :] * left)
+                    dirs[k + 1, c, plane, some, :] = (
+                        following[0] * dirs[k, c, plane, some, :]
+                        + following[1] * (inv[c, plane, some, :] * left)
                     )
 
-    def into_rbuf(c, plane, value):
-        rbuf[c, plane, own, :] = value
-
-    def from_rbuf(c, plane):
-        return rbuf[c, plane, own, :]
-
-    relax(0, lambda c, plane: rhs[c, plane, own, :], into_rbuf, steps[1])
-    start(dirs, (1,), "fine", 2, STAR)
+    BEYOND = ((1, 2, 3, 4), H - 1, rows + 2)
+    BLOCK = ((2, 3), H, rows)
+    relax(0, rhs, r2buf, steps[1], *BEYOND)
+    relax(1, r2buf, r2buf, steps[2], *BLOCK)
+    start(dirs, (2,), "fine", 2, STAR)
 
     lane = lane_of(ext)
     rid = lax.broadcasted_iota(jnp.int32, (ext, lanes), 0)
@@ -344,8 +358,8 @@
     def row_down(a):
         return pltpu.roll(a, 2, 0)
 
-    cmu = jnp.where(inside, 0.125 * cube_sum(coef[0, 2] + coef[0, 3]), 0.0)
-    clam = jnp.where(inside, 0.125 * cube_sum(coef[1, 2] + coef[1, 3]), 0.0)
+    cmu = jnp.where(inside, 0.125 * cube_sum(coef[0, 3] + coef[0, 4]), 0.0)
+    clam = jnp.where(inside, 0.125 * cube_sum(coef[1, 3] + coef[1, 4]), 0.0)
     cf = [
         0.5 * (cmu + row_up(cmu)),
         0.5 * (cmu + row_down(cmu)),
@@ -376,22 +390,20 @@
         return out
 
     for c in range(3):
-        for plane in (1, 2):
-            sol_ref[c, plane - 1] = dirs[0, c, plane, own, :] + dirs[1, c, plane, own, :]
-    arrive(dirs, (1,), "fine", 2, STAR)
-    relax(1, from_rbuf, into_rbuf, steps[2])
-    start(dirs, (2,), "fine", 3, STAR)
-    for c in range(3):
-        for plane in (1, 2):
-            sol_ref[c, plane - 1] += dirs[2, c, plane, own, :]
-    arrive(dirs, (2,), "fine", 3, STAR)
-    relax(2, from_rbuf, into_rbuf, None)
-    start(rbuf, (), "fine", 4, (2, 3, 0, 1, 4, 5, 6, 7))
+        for plane in (2, 3):
+            sol_ref[c, plane - 2] = (
+                dirs[0, c, plane, own, :]
+                + dirs[1, c, plane, own, :]
+                + dirs[2, c, plane, own, :]
+            )
+    arrive(dirs, (2,), "fine", 2, STAR)
+    relax(2, r2buf, rbuf, None, *BLOCK)
+    start(rbuf, (), "deep", 3, (2, 3, 0, 1, 4, 5, 6, 7))
 
     sub = lax.broadcasted_iota(jnp.int32, (8, lanes), 0)
     part = jnp.zeros((8, lanes), jnp.float32)
     for c in range(3):
-        both = rbuf[c, 1, own, :] + rbuf[c, 2, own, :]
+        both = rbuf[c, 2, own, :] + rbuf[c, 3, own, :]
         part = jnp.where(sub == c, jnp.sum(both, axis=0, keepdims=True), part)
     sums[0] = part
 
@@ -408,9 +420,9 @@
     for step in range(1, n_gy):
         sum_message(step).start()
 
-    arrive(rbuf, (), "fine", 4, (2, 3))
+    arrive(rbuf, (), "deep", 3, (2, 3))
     left = [
-        jnp.where(inside, cube_sum(rbuf[c, 1] + rbuf[c, 2]), 0.0) for c in range(3)
+        jnp.where(inside, cube_sum(rbuf[c, 2] + rbuf[c, 3]), 0.0) for c in range(3)
     ]
     coarse_steps = weights(COARSE_SWEEPS)
     direction = [coarse_steps[0][1] * cinv[c] * left[c] for c in range(3)]
@@ -436,46 +448,36 @@
     scale = jnp.full((8, 1), SHIFT_SCALE * cells_dev, jnp.float32) * members
     shift = jnp.sum(total, axis=1, keepdims=True) / scale
     for c in range(3):
-        fc[c, 1, own, :] = smoothed[c][H : H + rows] + shift[c : c + 1, :]
-    start(fc, (), "coarse", 5, ALL)
+        fc[c, 2, own, :] = smoothed[c][H : H + rows] + shift[c : c + 1, :]
+    start(fc, (), "coarse", 4, ALL)
     for c in range(3):
-        for plane in (1, 2):
-            sol_ref[c, plane - 1] += fc[c, 1, own, :]
-    arrive(rbuf, (), "fine", 4, (0, 1, 4, 5, 6, 7))
-    arrive(fc, (), "coarse", 5, ALL)
+        for plane in (2, 3):
+            sol_ref[c, plane - 2] += fc[c, 2, own, :]
+    arrive(rbuf, (), "deep", 3, (0, 1, 4, 5, 6, 7))
+    arrive(fc, (), "coarse", 4, ALL)
 
     def fc_load(c, plane, dp, dy):
-        return fc[c, (plane + 1 + dp) // 2, wide_first + dy : wide_first + dy + wide, :]
-
-    for plane in range(4):
+        return fc[c, (plane + 2 + dp) // 2, wide_first + dy : wide_first + dy + wide, :]
+
+    for plane in range(6):
         applied = operate(fc_load, plane, wide_first, wide)
         for c in range(3):
             value = rbuf[c, plane, wide_rows, :] - applied[c]
             r2buf[c, plane, wide_rows, :] = value
             dirs[3, c, plane, wide_rows, :] = steps[0][1] * inv[c, plane, wide_rows, :] * value
 
-    def into_r2(c, plane, value):
-        r2buf[c, plane, own, :] = value
-
-    def from_r2(c, plane):
-        return r2buf[c, plane, own, :]
-
-    def into_result(c, plane, value):
-        res_ref[c, plane - 1] = value
-
-    relax(3, from_r2, into_r2, steps[1])
-    start(dirs, (4,), "fine", 6, STAR)
+    relax(3, r2buf, r2buf, steps[1], *BEYOND)
+    relax(4, r2buf, r2buf, steps[2], *BLOCK)
+    start(dirs, (5,), "fine", 5, STAR)
     for c in range(3):
-        for plane in (1, 2):
-            sol_ref[c, plane - 1] += dirs[3, c, plane, own, :] + dirs[4, c, plane, own, :]
-    arrive(dirs, (4,), "fine", 6, STAR)
-    relax(4, from_r2, into_r2, steps[2])
-    start(dirs, (5,), "fine", 7, STAR)
-    for c in range(3):
-        for plane in (1, 2):
-            sol_ref[c, plane - 1] += dirs[5, c, plane, own, :]
-    arrive(dirs, (5,), "fine", 7, STAR)
-    relax(5, from_r2, into_result, None)
+        for plane in (2, 3):
+            sol_ref[c, plane - 2] += (
+                dirs[3, c, plane, own, :]
+                + dirs[4, c, plane, own, :]
+                + dirs[5, c, plane, own, :]
+            )
+    arrive(dirs, (5,), "fine", 5, STAR)
+    relax(5, r2buf, None, None, *BLOCK)
 
     for ref, lead, kind, round_id, way in started:
 
@@ -505,23 +507,23 @@
             in_specs=[hbm, hbm, hbm, hbm],
             out_specs=(vmem, vmem),
             scratch_shapes=[
-                pltpu.VMEM((2, 6, ext, lanes), f32),
-                pltpu.VMEM((3, 4, ext, lanes), f32),
-                pltpu.VMEM((3, 4, ext, lanes), f32),
-                pltpu.VMEM((6, 3, 4, ext, lanes), f32),
-                pltpu.VMEM((3, 4, ext, lanes), f32),
-                pltpu.VMEM((3, 4, ext, lanes), f32),
-                pltpu.VMEM((3, 3, ext, lanes), f32),
+                pltpu.VMEM((2, 8, ext, lanes), f32),
+                pltpu.VMEM((3, 6, ext, lanes), f32),
+                pltpu.VMEM((3, 6, ext, lanes), f32),
+                pltpu.VMEM((6, 3, 6, ext, lanes), f32),
+                pltpu.VMEM((3, 6, ext, lanes), f32),
+                pltpu.VMEM((3, 6, ext, lanes), f32),
+                pltpu.VMEM((3, 5, ext, lanes), f32),
                 pltpu.VMEM((n_gy, 8, lanes), f32),
                 pltpu.SMEM((1, n_gy), jnp.int32),
-                pltpu.SemaphoreType.DMA((8, 8)),
-                pltpu.SemaphoreType.DMA((8, 8)),
+                pltpu.SemaphoreType.DMA((6, 12)),
+                pltpu.SemaphoreType.DMA((6, 12)),
                 pltpu.SemaphoreType.DMA((n_gy,)),
                 pltpu.SemaphoreType.DMA((n_gy,)),
                 pltpu.SemaphoreType.DMA((4,)),
             ],
             compiler_params=pltpu.CompilerParams(
-                collective_id=0, has_side_effects=True, vmem_limit_bytes=24 * 1024 * 1024
+                collective_id=0, has_side_effects=True
             ),
             cost_estimate=pl.CostEstimate(
                 flops=10_000_000, bytes_accessed=400_000, transcendentals=0

time: 38.5 us -> 38.6 us (level)
  the two profiles are of different devices: /device:TPU:3 before, /device:TPU:0 now
where the time goes in v3:
time: 38.6 us; the launch traced here: 38.4 us
  Pallas kernels  35.5 us (92%)
  local copies, waits for them, and re-layouts  2.22 us (6%)
  between operations  0.65 us (2%)
    pallas_call x1, Pallas kernels, shards(): pl.pallas_call(functools.partial(kernel, n_gx, n_gy), out_shape=(field, f...  35.5 us
    unnamed x4, local copies, waits for them, and re-layouts  2.22 us

profile of v3, /device:TPU:0, one launch (start us, length us, event | category | flops | bytes accessed | tf_op | source)
XLA Modules:
  0.0 38.4 jit_solution(4974104823518530511)
XLA Ops:
  0.6 35.5 %shard_map.59 = (f32[3,2,32,128]{3,2,1,0:T(8,128)}, f32[3,2,32,128]{3,2,1,0:T(8,128)}) custom-call(f32[3,2,32,128]{3,2,1,0:T(8,128)} %rhs_in.1, f32[2,32,128]{2,1,0:T(8,128)} %mu_in.1, f32[2,32,128]{2,1,0:T(8,128)} %lam_in.1, s32[1,4]{1,0:T(1,128)} %starts_in.1), custom_call_target="tpu_custom_call" | custom-call | flops 10000000 | bytes 400000 | tf_op jit(solution)/shard_map/pallas_call | solution.py:504
  36.2 0.0 copy-start
  36.2 1.6 %copy.8 = f32[3,2,32,128]{3,2,1,0:T(8,128)} copy(f32[3,2,32,128]{3,2,1,0:T(8,128)} %get-tuple-element.4) | data formatting | bytes 196608
  37.8 0.0 copy-done
  37.8 0.6 %copy.9 = f32[3,2,32,128]{3,2,1,0:T(8,128)} copy(f32[3,2,32,128]{3,2,1,0:T(8,128)S(1)} %copy-done) | data formatting | bytes 196608
Async XLA Ops:
  36.2 1.6 %copy-start = (f32[3,2,32,128]{3,2,1,0:T(8,128)S(1)}, f32[3,2,32,128]{3,2,1,0:T(8,128)}, u32[]{:S(2)}) copy-start(f32[3,2,32,128]{3,2,1,0:T(8,128)} %get-tuple-element.5) | copy-start | bytes 294916

commit v4 on v2

--- a/solution.py
+++ b/solution.py
@@ -521,7 +521,7 @@
                 pltpu.SemaphoreType.DMA((4,)),
             ],
             compiler_params=pltpu.CompilerParams(
-                collective_id=0, has_side_effects=True, vmem_limit_bytes=24 * 1024 * 1024
+                collective_id=0, has_side_effects=True
             ),
             cost_estimate=pl.CostEstimate(
                 flops=10_000_000, bytes_accessed=400_000, transcendentals=0

time: 38.5 us -> 37 us (0.961)
  local copies, waits for them, and re-layouts: 4.34 us -> 2.22 us
  Pallas kernels: 33.2 us -> 34 us
    unnamed x10 -> x4, local copies, waits for them, and re-layouts: 4.34 us -> 2.22 us
    pallas_call x1, Pallas kernels: 33.2 us -> 34 us  [shards(): pl.pallas_call(functools.partial(kernel, n_gx, n_gy), out_shape=(field, f...]
where the time goes in v4:
time: 37 us; the launch traced here: 36.8 us
  Pallas kernels  34 us (92%)
  local copies, waits for them, and re-layouts  2.22 us (6%)
  between operations  0.65 us (2%)
    pallas_call x1, Pallas kernels, shards(): pl.pallas_call(functools.partial(kernel, n_gx, n_gy), out_shape=(field, f...  34 us
    unnamed x4, local copies, waits for them, and re-layouts  2.22 us

profile of v4, /device:TPU:3, one launch (start us, length us, event | category | flops | bytes accessed | tf_op | source)
XLA Modules:
  0.0 36.8 jit_solution(5738395716289399328)
XLA Ops:
  0.6 34.0 %shard_map.59 = (f32[3,2,32,128]{3,2,1,0:T(8,128)}, f32[3,2,32,128]{3,2,1,0:T(8,128)}) custom-call(f32[3,2,32,128]{3,2,1,0:T(8,128)} %rhs_in.1, f32[2,32,128]{2,1,0:T(8,128)} %mu_in.1, f32[2,32,128]{2,1,0:T(8,128)} %lam_in.1, s32[1,4]{1,0:T(1,128)} %starts_in.1), custom_call_target="tpu_custom_call" | custom-call | flops 10000000 | bytes 400000 | tf_op jit(solution)/shard_map/pallas_call | solution.py:502
  34.6 0.0 copy-start
  34.6 1.6 %copy.8 = f32[3,2,32,128]{3,2,1,0:T(8,128)} copy(f32[3,2,32,128]{3,2,1,0:T(8,128)} %get-tuple-element.4) | data formatting | bytes 196608
  36.2 0.0 copy-done
  36.2 0.6 %copy.9 = f32[3,2,32,128]{3,2,1,0:T(8,128)} copy(f32[3,2,32,128]{3,2,1,0:T(8,128)S(1)} %copy-done) | data formatting | bytes 196608
Async XLA Ops:
  34.6 1.6 %copy-start = (f32[3,2,32,128]{3,2,1,0:T(8,128)S(1)}, f32[3,2,32,128]{3,2,1,0:T(8,128)}, u32[]{:S(2)}) copy-start(f32[3,2,32,128]{3,2,1,0:T(8,128)} %get-tuple-element.5) | copy-start | bytes 294916

commit v5 on v4

--- a/solution.py
+++ b/solution.py
@@ -474,9 +474,6 @@
     for c in range(3):
         for plane in (1, 2):
             sol_ref[c, plane - 1] += dirs[5, c, plane, own, :]
-    arrive(dirs, (5,), "fine", 7, STAR)
-    relax(5, from_r2, into_result, None)
-
     for ref, lead, kind, round_id, way in started:
 
         @pl.when(exists(*DIRS[way]))
@@ -485,6 +482,9 @@
 
     for step in range(1, n_gy):
         sum_message(step).wait_send()
+
+    arrive(dirs, (5,), "fine", 7, STAR)
+    relax(5, from_r2, into_result, None)
 
 
 def solution(mesh):

time: 37 us -> 36.9 us (level)
  no operation moved by 1% of the time
where the time goes in v5:
time: 36.9 us; the launch traced here: 36.7 us
  Pallas kernels  33.9 us (92%)
  local copies, waits for them, and re-layouts  2.22 us (6%)
  between operations  0.65 us (2%)
    pallas_call x1, Pallas kernels, shards(): pl.pallas_call(functools.partial(kernel, n_gx, n_gy), out_shape=(field, f...  33.9 us
    unnamed x4, local copies, waits for them, and re-layouts  2.22 us

profile of v5, /device:TPU:3, one launch (start us, length us, event | category | flops | bytes accessed | tf_op | source)
XLA Modules:
  0.0 36.7 jit_solution(3885790525176562050)
XLA Ops:
  0.6 33.9 %shard_map.59 = (f32[3,2,32,128]{3,2,1,0:T(8,128)}, f32[3,2,32,128]{3,2,1,0:T(8,128)}) custom-call(f32[3,2,32,128]{3,2,1,0:T(8,128)} %rhs_in.1, f32[2,32,128]{2,1,0:T(8,128)} %mu_in.1, f32[2,32,128]{2,1,0:T(8,128)} %lam_in.1, s32[1,4]{1,0:T(1,128)} %starts_in.1), custom_call_target="tpu_custom_call" | custom-call | flops 10000000 | bytes 400000 | tf_op jit(solution)/shard_map/pallas_call | solution.py:502
  34.5 0.0 copy-start
  34.5 1.6 %copy.8 = f32[3,2,32,128]{3,2,1,0:T(8,128)} copy(f32[3,2,32,128]{3,2,1,0:T(8,128)} %get-tuple-element.4) | data formatting | bytes 196608
  36.1 0.0 copy-done
  36.1 0.6 %copy.9 = f32[3,2,32,128]{3,2,1,0:T(8,128)} copy(f32[3,2,32,128]{3,2,1,0:T(8,128)S(1)} %copy-done) | data formatting | bytes 196608
Async XLA Ops:
  34.5 1.6 %copy-start = (f32[3,2,32,128]{3,2,1,0:T(8,128)S(1)}, f32[3,2,32,128]{3,2,1,0:T(8,128)}, u32[]{:S(2)}) copy-start(f32[3,2,32,128]{3,2,1,0:T(8,128)} %get-tuple-element.5) | copy-start | bytes 294916

commit v6 on v5

--- a/solution.py
+++ b/solution.py
@@ -286,8 +286,24 @@
                 steps[0][1] * inv[c, plane, wide_rows, :] * rhs[c, plane, wide_rows, :]
             )
 
-    def relax(k, source, target, following):
-        for plane in (1, 2):
+    near_high = lax.rem(gx, 2) == 0
+
+    def relax(k, source, target, following, round_id=None):
+        for turn in range(2):
+            plane = turn + 1
+            if round_id is not None:
+                plane = jnp.where(near_high, 2 - turn, 1 + turn)
+                if turn == 0:
+                    arrive(dirs, (k,), "fine", round_id, (2, 3))
+                for way in (0, 1, 4, 5):
+                    sx, sy = DIRS[way]
+                    near = near_high if sx < 0 else jnp.logical_not(near_high)
+                    now = near if turn == 0 else jnp.logical_not(near)
+
+                    @pl.when(jnp.logical_and(now, exists(-sx, -sy)))
+                    def _(way=way):
+                        message(dirs, (k,), "fine", round_id, way).wait_recv()
+
             applied = operate(direction_load(k, H, rows), plane, H, rows)
             for c in range(3):
                 left = source(c, plane) - applied[c]
@@ -378,14 +394,12 @@
     for c in range(3):
         for plane in (1, 2):
             sol_ref[c, plane - 1] = dirs[0, c, plane, own, :] + dirs[1, c, plane, own, :]
-    arrive(dirs, (1,), "fine", 2, STAR)
-    relax(1, from_rbuf, into_rbuf, steps[2])
+    relax(1, from_rbuf, into_rbuf, steps[2], 2)
     start(dirs, (2,), "fine", 3, STAR)
     for c in range(3):
         for plane in (1, 2):
             sol_ref[c, plane - 1] += dirs[2, c, plane, own, :]
-    arrive(dirs, (2,), "fine", 3, STAR)
-    relax(2, from_rbuf, into_rbuf, None)
+    relax(2, from_rbuf, into_rbuf, None, 3)
     start(rbuf, (), "fine", 4, (2, 3, 0, 1, 4, 5, 6, 7))
 
     sub = lax.broadcasted_iota(jnp.int32, (8, lanes), 0)
@@ -468,8 +482,7 @@
     for c in range(3):
         for plane in (1, 2):
             sol_ref[c, plane - 1] += dirs[3, c, plane, own, :] + dirs[4, c, plane, own, :]
-    arrive(dirs, (4,), "fine", 6, STAR)
-    relax(4, from_r2, into_r2, steps[2])
+    relax(4, from_r2, into_r2, steps[2], 6)
     start(dirs, (5,), "fine", 7, STAR)
     for c in range(3):
         for plane in (1, 2):
@@ -483,8 +496,7 @@
     for step in range(1, n_gy):
         sum_message(step).wait_send()
 
-    arrive(dirs, (5,), "fine", 7, STAR)
-    relax(5, from_r2, into_result, None)
+    relax(5, from_r2, into_result, None, 7)
 
 
 def solution(mesh):

time: 36.9 us -> 36.9 us (level)
  no operation moved by 1% of the time
where the time goes in v6:
time: 36.9 us; the launch traced here: 36.7 us
  Pallas kernels  33.8 us (92%)
  local copies, waits for them, and re-layouts  2.22 us (6%)
  between operations  0.65 us (2%)
    pallas_call x1, Pallas kernels, shards(): pl.pallas_call(functools.partial(kernel, n_gx, n_gy), out_shape=(field, f...  33.8 us
    unnamed x4, local copies, waits for them, and re-layouts  2.22 us

profile of v6, /device:TPU:3, one launch (start us, length us, event | category | flops | bytes accessed | tf_op | source)
XLA Modules:
  0.0 36.7 jit_solution(1409876917825873665)
XLA Ops:
  0.6 33.8 %shard_map.59 = (f32[3,2,32,128]{3,2,1,0:T(8,128)}, f32[3,2,32,128]{3,2,1,0:T(8,128)}) custom-call(f32[3,2,32,128]{3,2,1,0:T(8,128)} %rhs_in.1, f32[2,32,128]{2,1,0:T(8,128)} %mu_in.1, f32[2,32,128]{2,1,0:T(8,128)} %lam_in.1, s32[1,4]{1,0:T(1,128)} %starts_in.1), custom_call_target="tpu_custom_call" | custom-call | flops 10000000 | bytes 400000 | tf_op jit(solution)/shard_map/pallas_call | solution.py:514
  34.5 0.0 copy-start
  34.5 1.6 %copy.8 = f32[3,2,32,128]{3,2,1,0:T(8,128)} copy(f32[3,2,32,128]{3,2,1,0:T(8,128)} %get-tuple-element.4) | data formatting | bytes 196608
  36.1 0.0 copy-done
  36.1 0.6 %copy.9 = f32[3,2,32,128]{3,2,1,0:T(8,128)} copy(f32[3,2,32,128]{3,2,1,0:T(8,128)S(1)} %copy-done) | data formatting | bytes 196608
Async XLA Ops:
  34.5 1.6 %copy-start = (f32[3,2,32,128]{3,2,1,0:T(8,128)S(1)}, f32[3,2,32,128]{3,2,1,0:T(8,128)}, u32[]{:S(2)}) copy-start(f32[3,2,32,128]{3,2,1,0:T(8,128)} %get-tuple-element.5) | copy-start | bytes 294916
